TPU v7x, 32 devices: a whole 2x2x4 slice. The times are simulated.
32 devices in a mesh: dp: 8 (over z, x), tensor: 4 (over y, core).
Axes of the slice: x: 2, y: 2, z: 4, core: 2. Of those that a mesh axis runs over, the one named last changes fastest.
Arguments:
- hidden: bfloat16 [2048, 8192], P('dp', 'tensor'), may hold values from -6 to 6
- connector: bfloat16 [8192, 3584], P('tensor'), may hold values from -0.0625 to 0.0625
- routing: int32 [2048, 1], P('dp'), may hold values from 0 to 3; in each aligned block of 256 rows (0 to 255, 256 to 511, ...) at most 128 rows name the same one
- talker_in: bfloat16 [4096, 3584], P(('dp', 'tensor')), may hold values from -6 to 6
- norm_gain: float32 [3584], replicated, may hold values from 0.25 to 1.75
- kv_weight: bfloat16 [3584, 1024], replicated, may hold values from -0.09375 to 0.09375
- kv_grad: bfloat16 [4096, 1024], P(('dp', 'tensor')), may hold values from -6 to 6
Outputs:
- hidden_grad: bfloat16 [2048, 8192], P('dp', 'tensor')
- connector_grad: float32 [8192, 3584], P('tensor', 'dp')
- kv_weight_grad: float32 [3584, 1024], P(None, ('dp', 'tensor'))
Inputs may be any that keep to these rules, and one draw needn't show every extreme that they name: `routing`: among the 256 rows of one index of dp, at most 128 go to one shard.
All inputs are finite; a program needn't handle non-finite values.
Results may differ from a plain program's by a relative error of at most 0.005.
Values may be sent and summed in bfloat16 or wider, within the bound.
No kernel may reach another device: no remote copies, remote signals or barrier semaphores. Data moves between devices by JAX's collectives and lax.ppermute only.
A program may use at most 128 MiB of HBM per device.

v0:
```python
import math

import jax
import jax.numpy as jnp
from jax import lax
from jax.sharding import PartitionSpec as P

CONTRACT_LAST = (((1,), (1,)), ((), ()))
CONTRACT_FIRST = (((0,), (0,)), ((), ()))


def on_device(hidden, connector, routing, talker_in, norm_gain, kv_weight, kv_grad):
    dp_count = lax.axis_size("dp")
    tensor_count = lax.axis_size("tensor")
    rows_dev = hidden.shape[0]
    capacity = talker_in.shape[0]
    factor = 1.0 / math.sqrt(rows_dev * dp_count)
    route_rows = routing[:, 0]
    shards = jnp.arange(tensor_count, dtype=jnp.int32)
    onehot = (route_rows[:, None] == shards[None, :]).astype(jnp.int32)
    ranks = jnp.sum((jnp.cumsum(onehot, axis=0) - 1) * onehot, axis=1)
    slot_ids = route_rows * capacity + ranks
    counts = jnp.sum(onehot, axis=0)
    tensor_pos = lax.axis_index("tensor")
    own_count = jnp.sum(jnp.where(shards == tensor_pos, counts, 0))
    usable = jnp.arange(capacity, dtype=jnp.int32) < own_count
    masked = jnp.where(usable[:, None], kv_grad, jnp.zeros_like(kv_grad))
    inputs = talker_in.astype(jnp.float32)
    inv_rms = lax.rsqrt(jnp.mean(inputs * inputs, axis=1, keepdims=True) + 1e-06)
    scaled = inputs * inv_rms
    normed = (scaled * norm_gain).astype(jnp.bfloat16)
    back_grad = lax.dot_general(
        masked, kv_weight, CONTRACT_LAST, preferred_element_type=jnp.float32
    )
    gain_back = norm_gain * back_grad
    talker_grad = (
        inv_rms * (gain_back - scaled * jnp.mean(gain_back * scaled, axis=1, keepdims=True))
    ).astype(jnp.bfloat16)
    col_count = masked.shape[1]
    per_dev = col_count // (dp_count * tensor_count)
    group_rows = lax.all_gather(normed, "tensor", axis=0, tiled=True)
    regrouped = masked.reshape(capacity, dp_count, tensor_count, per_dev)
    regrouped = regrouped.transpose(0, 2, 1, 3).reshape(capacity, col_count)
    group_cols = lax.all_to_all(regrouped, "tensor", split_axis=1, concat_axis=0, tiled=True)
    block_terms = (
        lax.dot_general(group_rows, group_cols, CONTRACT_FIRST, preferred_element_type=jnp.float32)
        * factor
    )
    kv_weight_grad = lax.psum_scatter(block_terms, "dp", scatter_dimension=1, tiled=True)
    gathered = lax.all_gather(talker_grad, "tensor", axis=0, tiled=True)
    row_grad = jnp.take(gathered, slot_ids, axis=0)
    hidden_grad = lax.dot_general(
        row_grad, connector, CONTRACT_LAST, preferred_element_type=jnp.float32
    ).astype(jnp.bfloat16)
    conn_terms = (
        lax.dot_general(hidden, row_grad, CONTRACT_FIRST, preferred_element_type=jnp.float32)
        * factor
    )
    connector_grad = lax.psum_scatter(conn_terms, "dp", scatter_dimension=1, tiled=True)
    return (hidden_grad, connector_grad, kv_weight_grad)


def solution(mesh):
    return jax.shard_map(
        on_device,
        mesh=mesh,
        in_specs=(
            P("dp", "tensor"),
            P("tensor", None),
            P("dp", None),
            P(("dp", "tensor"), None),
            P(),
            P(),
            P(("dp", "tensor"), None),
        ),
        out_specs=(P("dp", "tensor"), P("tensor", "dp"), P(None, ("dp", "tensor"))),
        check_vma=False,
    )
```

profile of v0, /device:TPU:0, one launch (start us, length us, event | category | flops | bytes accessed | tf_op | source)
XLA Modules:
  0.0 649.9 jit_solution(14165404675179795144)
XLA Ops:
  7.3 1.6 fusion.8
  8.8 0.7 compare_convert_fusion
  9.5 1.2 reduce-window.6
  10.8 0.1 copy.12
  11.0 0.1 copy.13
  11.1 0.8 fusion.10
  11.9 0.6 fusion.11
  12.6 0.6 iota_compare_fusion.1
  13.2 1.1 copy.14
  14.4 5.8 fusion.3
  20.2 1.8 fusion.7
  22.1 0.7 all-gather.3.cloned.1.call-update
  22.8 10.1 %all_to_all.19 = bf16[128,4,256]{0,2,1:T(8,128)(2,1)S(1)} all-to-all(bf16[128,4,256]{0,2,1:T(8,128)(2,1)S(1)} %bitcast.35), channel_id=1, replica_groups=mesh['dp'=8,'tensor'=4] {'tensor'}, dimensions={1} | all-to-all | bytes 524288 | tf_op jit(solution)/shard_map/all_to_all | solution.py:44
  32.9 0.1 copy.16
  33.1 23.3 %all-gather.5.cloned.1.call-done = bf16[512,3584]{1,0:T(8,128)(2,1)} async-done(((bf16[128,3584]{1,0:T(8,128)(2,1)}), bf16[512,3584]{1,0:T(8,128)(2,1)}) %all-gather.5.cloned.1.call-update) | async-done | bytes 3670032 | tf_op jit(solution)/shard_map/all_gather | solution.py:41
  56.4 5.0 convolution_multiply_fusion
  61.4 0.2 reduce-scatter.3.cloned.1.call-start
  61.7 0.4 copy-done.4
  62.1 28.0 %all-gather.3.cloned.1.call-done = bf16[512,3584]{1,0:T(8,128)(2,1)} async-done(((bf16[128,3584]{1,0:T(8,128)(2,1)}), bf16[512,3584]{1,0:T(8,128)(2,1)}) %all-gather.3.cloned.1.call-update) | async-done | bytes 3670032 | tf_op jit(solution)/shard_map/all_gather | solution.py:50
  90.1 6.0 gather_fusion
  96.1 12.2 %multiply_bitcast_fusion = f32[2048,3584]{0,1:T(8,128)} fusion(bf16[256,2048]{1,0:T(8,128)(2,1)S(1)} %copy-done, bf16[256,3584]{1,0:T(8,128)(2,1)S(1)} %gather_fusion, pred[256]{0:T(512)(128)(4,1)S(1)} %get-tuple-element.5), kind=kOutput, calls=%fused_computation.1 | convolution fusion | flops 3766353920 | bytes 32243968 | tf_op jit(solution)/shard_map/dot_general | solution.py:56
  108.3 8.6 %convolution_convert_fusion = bf16[256,2048]{1,0:T(8,128)(2,1)} fusion(bf16[2048,3584]{1,0:T(8,128)(2,1)} %param.8, bf16[256,3584]{1,0:T(8,128)(2,1)S(1)} %gather_fusion, pred[256]{0:T(512)(128)(4,1)S(1)} %get-tuple-element.5), kind=kOutput, calls=%fused_computation.4 | convolution fusion | flops 3759538176 | bytes 17563904 | tf_op jit(solution)/shard_map/dot_general | solution.py:52
  117.0 58.3 %reduce-scatter.5.cloned.1.call-done = f32[3584,32]{0,1:T(8,128)} async-done(((f32[3584,256]{0,1:T(8,128)}), f32[3584,32]{0,1:T(8,128)}) %reduce-scatter.5.cloned.1.call-update) | async-done | bytes 458768 | tf_op jit(solution)/shard_map/reduce_scatter | solution.py:49
  175.2 468.2 %reduce-scatter.3.cloned.1.call-done = f32[2048,448]{0,1:T(8,128)} async-done(((f32[2048,3584]{0,1:T(8,128)}), f32[2048,448]{0,1:T(8,128)}) %reduce-scatter.3.cloned.1.call-update) | async-done | bytes 3670032 | tf_op jit(solution)/shard_map/reduce_scatter | solution.py:59
  (25 shorter events, 0.5 us)
Async XLA Ops:
  7.2 89.0 %copy-start = (bf16[256,2048]{1,0:T(8,128)(2,1)S(1)}, bf16[256,2048]{1,0:T(8,128)(2,1)}, u32[]{:S(2)}) copy-start(bf16[256,2048]{1,0:T(8,128)(2,1)} %param.7) | copy-start | bytes 3145732
  7.2 7.2 %copy-start.2 = (bf16[128,3584]{1,0:T(8,128)(2,1)S(1)}, bf16[128,3584]{1,0:T(8,128)(2,1)}, u32[]{:S(2)}) copy-start(bf16[128,3584]{1,0:T(8,128)(2,1)} %param.10) | copy-start | bytes 2752516
  7.2 7.2 %copy-start.3 = (f32[3584]{0:T(1024)S(1)}, f32[3584]{0:T(1024)}, u32[]{:S(2)}) copy-start(f32[3584]{0:T(1024)} %param.11) | copy-start | bytes 43012
  7.2 49.2 %all-gather.5.cloned.1.call-start = ((), (), s32[]{:S(2)}) async-start(), calls=%async_computation.5 | async-start | bytes 4587520 | tf_op jit(solution)/shard_map/all_gather | solution.py:41
  22.0 68.0 %all-gather.3.cloned.1.call-start = ((), (), s32[]{:S(2)}) async-start(), calls=%async_computation.3 | async-start | bytes 4587520 | tf_op jit(solution)/shard_map/all_gather | solution.py:50
  22.8 152.4 %reduce-scatter.5.cloned.1.call-start = ((), (), s32[]{:S(2)}) async-start(), calls=%async_computation.6 | async-start | bytes 4128768 | tf_op jit(solution)/shard_map/reduce_scatter | solution.py:49
  61.4 0.7 copy-start.4
  61.4 582.0 %reduce-scatter.3.cloned.1.call-start = ((), (), s32[]{:S(2)}) async-start(), calls=%async_computation.4 | async-start | bytes 33030144 | tf_op jit(solution)/shard_map/reduce_scatter | solution.py:59
  108.3 535.1 %copy-start.1 = (bf16[256,2048]{1,0:T(8,128)(2,1)S(1)}, bf16[256,2048]{1,0:T(8,128)(2,1)}, u32[]{:S(2)}) copy-start(bf16[256,2048]{1,0:T(8,128)(2,1)} %param.7) | copy-start | bytes 3145732
Sparse Core Ops, SparseCore 0:
  22.1 34.1 all-gather.4
  58.5 31.4 all-gather.2
  94.3 80.8 reduce-scatter.4
  179.5 463.8 reduce-scatter.2
where the time goes:
time: 650 us
  waiting for transfers between devices  578 us (89%)
  matrix products  31.6 us (5%)
  between operations  13.9 us (2%)
  blocking collectives  10.1 us (2%)
  local copies, waits for them, and re-layouts  8.06 us (1%)
  other arithmetic  7.52 us (1%)
    reduce_scatter x1, waiting for transfers between devices, on_device(): lax.psum_scatter(conn_terms, 'dp', scatter_dimension=1, tiled=True)  468 us
    reduce_scatter x1, waiting for transfers between devices, on_device(): lax.psum_scatter(block_terms, 'dp', scatter_dimension=1, tiled=True)  58.3 us
    all_gather x1, waiting for transfers between devices, on_device(): gathered = lax.all_gather(talker_grad, 'tensor', axis=0, tiled=True)  28 us
    all_gather x1, waiting for transfers between devices, on_device(): group_rows = lax.all_gather(normed, 'tensor', axis=0, tiled=True)  23.3 us
  transfers between devices with their start and end apart: 4, of which 4 were waited for; matrix products, arithmetic and copies ran while one was open for 5% of the time, Pallas kernels for 0%

commit v1 on v0

v1 whole, which is shorter than its diff:
```python
import math

import jax
import jax.numpy as jnp
from jax import lax
from jax.sharding import PartitionSpec as P

CONTRACT_LAST = (((1,), (1,)), ((), ()))
CONTRACT_FIRST = (((0,), (0,)), ((), ()))
ROWS_BY_COLS = (((1,), (0,)), ((), ()))
CHUNKS = 4
F32 = jnp.float32
BF16 = jnp.bfloat16


def dot(a, b, dims):
    return lax.dot_general(a, b, dims, preferred_element_type=F32)


def strides_of(count):
    found = []
    step = count // 2
    while step:
        found.append(step)
        step //= 2
    return found


def bit_reverse(index, count):
    out = jnp.zeros_like(index)
    for place, step in enumerate(strides_of(count)):
        out = out + ((index // step) % 2) * (1 << place)
    return out


def on_device(hidden, connector, routing, talker_in, norm_gain, kv_weight, kv_grad):
    dp_count = lax.axis_size("dp")
    tensor_count = lax.axis_size("tensor")
    pair = 2 if dp_count % 2 == 0 else 1
    line = dp_count // pair
    rows_dev, width = hidden.shape
    capacity, features = talker_in.shape
    kv_cols = kv_grad.shape[1]
    factor = 1.0 / math.sqrt(rows_dev * dp_count)
    dp_pos = lax.axis_index("dp")
    tensor_pos = lax.axis_index("tensor")
    line_pos, pair_pos = dp_pos // pair, dp_pos % pair
    steps = strides_of(tensor_count)

    def tensor_swap(array, step):
        return lax.ppermute(array, "tensor", [(i, i ^ step) for i in range(tensor_count)])

    def pair_swap(array):
        return lax.ppermute(array, "dp", [(i, i ^ 1) for i in range(dp_count)])

    def line_shift(array, by):
        moves = [(i, ((i // pair + by) % line) * pair + i % pair) for i in range(dp_count)]
        return lax.ppermute(array, "dp", moves)

    chunk = width // CHUNKS
    held = []
    for c in range(CHUNKS):
        block = hidden[:, c * chunk:(c + 1) * chunk]
        blocks = [block]
        for _ in range(line - 1):
            block = line_shift(block, 1)
            blocks.append(block)
        held.append(blocks)

    def tensor_blocks(array):
        found = {0: array}
        for step in steps:
            for d in list(found):
                found[d ^ step] = tensor_swap(found[d], step)
        return found

    kv_blocks = tensor_blocks(kv_grad)
    in_blocks = tensor_blocks(talker_in)
    order = sorted(in_blocks)

    route_rows = routing[:, 0]
    earlier = jnp.arange(rows_dev)[None, :] < jnp.arange(rows_dev)[:, None]
    same = route_rows[:, None] == route_rows[None, :]
    ranks = jnp.sum((same & earlier).astype(jnp.int32), axis=1)
    spot = jnp.zeros_like(route_rows)
    for place, d in enumerate(order):
        spot = jnp.where(route_rows == (tensor_pos ^ d), place * capacity + ranks, spot)
    pick = (spot[:, None] == jnp.arange(tensor_count * capacity)[None, :]).astype(BF16)

    kv_all = jnp.concatenate([kv_blocks[d] for d in order], axis=0)
    in_all = jnp.concatenate([in_blocks[d] for d in order], axis=0)
    masked = dot(pick, kv_all, ROWS_BY_COLS).astype(BF16)
    inputs = dot(pick, in_all, ROWS_BY_COLS)

    inv_rms = lax.rsqrt(jnp.mean(inputs * inputs, axis=1, keepdims=True) + 1e-06)
    scaled = inputs * inv_rms
    normed = (scaled * norm_gain).astype(BF16)
    gain_back = norm_gain * dot(masked, kv_weight, CONTRACT_LAST)
    row_grad = (
        inv_rms * (gain_back - scaled * jnp.mean(gain_back * scaled, axis=1, keepdims=True))
    ).astype(BF16)

    share = rows_dev // tensor_count
    cols = features // dp_count
    mine = lax.dynamic_slice_in_dim(row_grad, bit_reverse(tensor_pos, tensor_count) * share, share, 0)
    mine = mine.reshape(share, dp_count, cols).transpose(1, 0, 2)
    got = []
    for s in range(line):
        target = ((line_pos + s) % line) * pair
        piece = jnp.stack([
            lax.dynamic_index_in_dim(mine, target + (pair_pos + o) % pair, 0, keepdims=False)
            for o in range(pair)
        ])
        got.append(line_shift(piece, s) if s else piece)
    shared = jnp.stack(got, axis=1)
    for step in steps:
        other = tensor_swap(shared, step)
        low = (tensor_pos // step) % 2 == 0
        shared = jnp.where(
            low,
            jnp.concatenate([shared, other], axis=2),
            jnp.concatenate([other, shared], axis=2),
        )
    sides = shared.reshape(pair, line * rows_dev, cols)

    per_dev = kv_cols // (dp_count * tensor_count)
    masked_t = masked.T.reshape(dp_count, tensor_count, per_dev, rows_dev)
    masked_t = lax.dynamic_index_in_dim(masked_t, tensor_pos, 1, keepdims=False)
    terms = dot(masked_t.reshape(dp_count * per_dev, rows_dev), normed, ROWS_BY_COLS) * factor
    terms = terms.reshape(line, pair, per_dev, features)
    own_terms = lax.dynamic_index_in_dim(terms, pair_pos, 1, keepdims=False)
    if pair == 2:
        far_terms = lax.dynamic_index_in_dim(terms, 1 - pair_pos, 1, keepdims=False)
        own_terms = own_terms + pair_swap(far_terms.astype(BF16)).astype(F32)
    kv_out = lax.dynamic_index_in_dim(own_terms, line_pos, 0, keepdims=False)
    for s in range(1, line):
        piece = lax.dynamic_index_in_dim(own_terms, (line_pos + s) % line, 0, keepdims=False)
        kv_out = kv_out + line_shift(piece.astype(BF16), s).astype(F32)
    kv_weight_grad = kv_out.T

    hidden_grad = dot(row_grad, connector, CONTRACT_LAST).astype(BF16)

    outs = []
    for blocks in held:
        rows = jnp.concatenate(blocks, axis=0)
        total = dot(rows, sides[0], CONTRACT_FIRST) * factor
        if pair == 2:
            far = (dot(rows, sides[1], CONTRACT_FIRST) * factor).astype(BF16)
            total = total + pair_swap(far).astype(F32)
        outs.append(total)
    connector_grad = jnp.concatenate(outs, axis=0)
    return (hidden_grad, connector_grad, kv_weight_grad)


def solution(mesh):
    return jax.shard_map(
        on_device,
        mesh=mesh,
        in_specs=(
            P("dp", "tensor"),
            P("tensor", None),
            P("dp", None),
            P(("dp", "tensor"), None),
            P(),
            P(),
            P(("dp", "tensor"), None),
        ),
        out_specs=(P("dp", "tensor"), P("tensor", "dp"), P(None, ("dp", "tensor"))),
        check_vma=False,
    )
```

time: 650 us -> 196 us (0.30)
  waiting for transfers between devices: 578 us -> 108 us
  starting transfers between devices: 0.34 us -> 33.9 us
  between operations: 13.9 us -> 1.26 us
  blocking collectives: 10.1 us -> 0 us
    reduce_scatter x2 -> x0, waiting for transfers between devices: 526 us -> none  [the longest x1 468 us: on_device(): lax.psum_scatter(conn_terms, 'dp', scatter_dimension=1, tiled=True)]
    ppermute x0 -> x31, waiting for transfers between devices: none -> 108 us  [the longest x18 50.1 us: line_shift(): return lax.ppermute(array, 'dp', moves)]
    all_gather x2 -> x0, waiting for transfers between devices: 51.3 us -> none  [the longest x1 28 us: on_device(): gathered = lax.all_gather(talker_grad, 'tensor', axis=0, tiled=True)]
    ppermute x0 -> x31, starting transfers between devices: none -> 33.9 us  [the longest x18 22.9 us: line_shift(): return lax.ppermute(array, 'dp', moves)]
    all_to_all x1 -> x0, blocking collectives: 10.1 us -> none  [on_device(): lax.all_to_all(regrouped, 'tensor', split_axis=1, concat_axis=0, tiled=True)]
    dot_general x4 -> x13, matrix products: 31.6 us -> 30.4 us  [dot(): return lax.dot_general(a, b, dims, preferred_element_type=F32)]
  transfers between devices with their start and end apart: 4 -> 31, of which waited for: 4 -> 12; matrix products, arithmetic and copies ran while one was open for 5% -> 24% of each run, Pallas kernels for 0% -> 0%
where the time goes in v1:
time: 196 us; the launch traced here: 195 us
  waiting for transfers between devices  108 us (55%)
  starting transfers between devices  33.9 us (17%)
  matrix products  30.4 us (16%)
  local copies, waits for them, and re-layouts  13.9 us (7%)
  other arithmetic  7.92 us (4%)
    ppermute x18, waiting for transfers between devices, line_shift(): return lax.ppermute(array, 'dp', moves)  50.1 us
    ppermute x8, waiting for transfers between devices, tensor_swap(): lax.ppermute(array, 'tensor', [(i, i ^ step) for i in range(tensor_count)])  30.8 us
    dot_general x13, matrix products, dot(): return lax.dot_general(a, b, dims, preferred_element_type=F32)  30.4 us
    ppermute x5, waiting for transfers between devices, pair_swap(): return lax.ppermute(array, 'dp', [(i, i ^ 1) for i in range(dp_count)])  26.8 us
    ppermute x18, starting transfers between devices, line_shift(): return lax.ppermute(array, 'dp', moves)  22.9 us
    ppermute x5, starting transfers between devices, pair_swap(): return lax.ppermute(array, 'dp', [(i, i ^ 1) for i in range(dp_count)])  5.79 us
    ppermute x8, starting transfers between devices, tensor_swap(): lax.ppermute(array, 'tensor', [(i, i ^ step) for i in range(tensor_count)])  5.21 us
  transfers between devices with their start and end apart: 31, of which 12 were waited for; matrix products, arithmetic and copies ran while one was open for 24% of the time, Pallas kernels for 0%

profile of v1, /device:TPU:0, one launch (start us, length us, event | category | flops | bytes accessed | tf_op | source)
XLA Modules:
  0.0 195.2 jit_solution(9616320161495067301)
XLA Ops:
  0.7 3.0 %collective-permute-start.1 = (bf16[128,3584]{1,0:T(8,128)(2,1)}, bf16[128,3584]{1,0:T(8,128)(2,1)}, u32[]{:S(2)}, u32[]{:S(2)}) collective-permute-start(bf16[128,3584]{1,0:T(8,128)(2,1)} %param.10), channel_id=1, source_target_pairs={{0,2},{1,3},{2,0},{3,1},{4,6},{5,7},{6,4},{7,5},{8,10},{9,11},{10,... | collective-permute-start | bytes 2752520 | tf_op jit(solution)/shard_map/ppermute | solution.py:51
  4.3 20.9 %collective-permute-done.1 = bf16[128,3584]{1,0:T(8,128)(2,1)} collective-permute-done((bf16[128,3584]{1,0:T(8,128)(2,1)}, bf16[128,3584]{1,0:T(8,128)(2,1)}, u32[]{:S(2)}, u32[]{:S(2)}) %collective-permute-start.1) | collective-permute-done | bytes 917536 | tf_op jit(solution)/shard_map/ppermute | solution.py:51
  25.2 2.1 %fusion.46 = (bf16[256,512]{1,0:T(8,128)(2,1)}, bf16[256,512]{1,0:T(8,128)(2,1)}, bf16[256,512]{1,0:T(8,128)(2,1)S(1)}, bf16[256,512]{1,0:T(8,128)(2,1)}) fusion(bf16[256,2048]{1,0:T(8,128)(2,1)} %param.7), kind=kLoop, calls=%fused_computation.107 | loop fusion | bytes 2097152 | tf_op jit(solution)/shard_map/slice | solution.py:63
  27.3 2.1 %collective-permute-start.6 = (bf16[256,512]{1,0:T(8,128)(2,1)}, bf16[256,512]{1,0:T(8,128)(2,1)}, u32[]{:S(2)}, u32[]{:S(2)}) collective-permute-start(bf16[256,512]{1,0:T(8,128)(2,1)} %get-tuple-element.8), channel_id=1, source_target_pairs={{0,8},{4,12},{8,16},{12,20},{16,24},{20,28},{24,0},{28,4},{1,9},{5... | collective-permute-start | bytes 786440 | tf_op jit(solution)/shard_map/ppermute | solution.py:58
  35.0 2.2 %copy.23 = bf16[1024,256]{1,0:T(8,128)(2,1)} copy(bf16[1024,256]{0,1:T(8,128)(2,1)} %bitcast.71) | data formatting | bytes 1048576 | tf_op jit(solution)/shard_map/convert_element_type | solution.py:92
  39.8 3.0 %multiply_reduce_fusion.1 = (f32[256]{0:T(256)S(1)}, f32[256,3584]{1,0:T(8,128)S(1)}) fusion(bf16[128,3584]{1,0:T(8,128)(2,1)} %collective-permute-done.2, bf16[128,3584]{1,0:T(8,128)(2,1)} %collective-permute-done.1, bf16[128,3584]{1,0:T(8,128)(2,1)} %collective-permute-done, bf16[128,3584]{1,0:T(8,128)(2,1)} %param.10, s32[256]{0:T(256)S(1)} %bitcast.91), kind=kOutput, calls=%fused_computation.14 | convolution fusion | flops 956169984 | bytes 7342080 | tf_op jit(solution)/shard_map/dot_general | solution.py:17
  47.2 2.4 %multiply_reduce_fusion = (f32[256]{0:T(256)S(1)}, f32[256,3584]{1,0:T(8,128)S(1)}) fusion(f32[256,3584]{1,0:T(8,128)S(1)} %get-tuple-element.21, f32[256]{0:T(256)S(1)} %add_rsqrt_fusion, bf16[256,1024]{1,0:T(8,128)(2,1)S(1)} %copy-done.2, bf16[3584,1024]{1,0:T(8,128)(2,1)S(1)} %bitcast.70, f32[3584]{0:T(1024)S(1)} %copy-done.3), kind=kOutput, calls=%fused_computation.13 | convolution fusion | flops 1882717952 | bytes 15220736 | tf_op jit(solution)/shard_map/dot_general | solution.py:17
  51.3 8.4 %convolution_convert_fusion = bf16[256,2048]{1,0:T(8,128)(2,1)} fusion(bf16[256,3584]{1,0:T(8,128)(2,1)S(1)} %multiply_convert_fusion.1, bf16[2048,3584]{1,0:T(8,128)(2,1)} %param.8), kind=kOutput, calls=%fused_computation.15 | convolution fusion | flops 3758620672 | bytes 17563648 | tf_op jit(solution)/shard_map/dot_general | solution.py:17
  66.2 3.4 %collective-permute-done.9 = bf16[2,64,448]{2,1,0:T(8,128)(2,1)S(1)} collective-permute-done((bf16[2,64,448]{2,1,0:T(8,128)(2,1)S(1)}, bf16[2,64,448]{2,1,0:T(8,128)(2,1)S(1)}, u32[]{:S(2)}, u32[]{:S(2)}) %collective-permute-start.9) | collective-permute-done | bytes 114720 | tf_op jit(solution)/shard_map/ppermute | solution.py:58
  71.2 19.1 %collective-permute-done.10 = bf16[2,64,448]{2,1,0:T(8,128)(2,1)S(1)} collective-permute-done((bf16[2,64,448]{2,1,0:T(8,128)(2,1)S(1)}, bf16[2,64,448]{2,1,0:T(8,128)(2,1)S(1)}, u32[]{:S(2)}, u32[]{:S(2)}) %collective-permute-start.10) | collective-permute-done | bytes 114720 | tf_op jit(solution)/shard_map/ppermute | solution.py:58
  90.4 3.3 %collective-permute-start.24 = (bf16[256,512]{1,0:T(8,128)(2,1)}, bf16[256,512]{1,0:T(8,128)(2,1)}, u32[]{:S(2)}, u32[]{:S(2)}) collective-permute-start(bf16[256,512]{1,0:T(8,128)(2,1)} %collective-permute-done.23), channel_id=1, source_target_pairs={{0,8},{4,12},{8,16},{12,20},{16,24},{20,28},{24,0},{28,4},{1,9},{5... | collective-permute-start | bytes 786440 | tf_op jit(solution)/shard_map/ppermute | solution.py:58
  98.9 8.5 %collective-permute-done.12 = bf16[2,4,64,448]{3,2,0,1:T(8,128)(2,1)S(1)} collective-permute-done((bf16[2,4,64,448]{3,2,0,1:T(8,128)(2,1)S(1)}, bf16[2,4,64,448]{3,2,0,1:T(8,128)(2,1)S(1)}, u32[]{:S(2)}, u32[]{:S(2)}) %collective-permute-start.12) | collective-permute-done | bytes 458784 | tf_op jit(solution)/shard_map/ppermute | solution.py:51
  109.1 2.0 %collective-permute-start.8 = (bf16[256,512]{1,0:T(8,128)(2,1)}, bf16[256,512]{1,0:T(8,128)(2,1)}, u32[]{:S(2)}, u32[]{:S(2)}) collective-permute-start(bf16[256,512]{1,0:T(8,128)(2,1)} %copy-done.8), channel_id=1, source_target_pairs={{0,8},{4,12},{8,16},{12,20},{16,24},{20,28},{24,0},{28,4},{1,9},{5... | collective-permute-start | bytes 786440 | tf_op jit(solution)/shard_map/ppermute | solution.py:58
  111.5 6.7 %collective-permute-done.29 = bf16[32,3584]{1,0:T(8,128)(2,1)} collective-permute-done((bf16[32,3584]{1,0:T(8,128)(2,1)}, bf16[32,3584]{1,0:T(8,128)(2,1)}, u32[]{:S(2)}, u32[]{:S(2)}) %collective-permute-start.29) | collective-permute-done | bytes 229408 | tf_op jit(solution)/shard_map/ppermute | solution.py:58
  118.2 2.3 %collective-permute-start.25 = (bf16[256,512]{1,0:T(8,128)(2,1)}, bf16[256,512]{1,0:T(8,128)(2,1)}, u32[]{:S(2)}, u32[]{:S(2)}) collective-permute-start(bf16[256,512]{1,0:T(8,128)(2,1)} %collective-permute-done.24), channel_id=1, source_target_pairs={{0,8},{4,12},{8,16},{12,20},{16,24},{20,28},{24,0},{28,4},{1,9},{5... | collective-permute-start | bytes 786440 | tf_op jit(solution)/shard_map/ppermute | solution.py:58
  120.5 20.8 %collective-permute-done.30 = bf16[32,3584]{1,0:T(8,128)(2,1)} collective-permute-done((bf16[32,3584]{1,0:T(8,128)(2,1)}, bf16[32,3584]{1,0:T(8,128)(2,1)}, u32[]{:S(2)}, u32[]{:S(2)}) %collective-permute-start.30) | collective-permute-done | bytes 229408 | tf_op jit(solution)/shard_map/ppermute | solution.py:58
  141.3 1.9 fusion.28
  153.0 1.9 fusion.16
  158.9 3.6 %collective-permute-done.14 = bf16[512,448]{0,1:T(8,128)(2,1)S(1)} collective-permute-done((bf16[512,448]{0,1:T(8,128)(2,1)S(1)}, bf16[512,448]{0,1:T(8,128)(2,1)S(1)}, u32[]{:S(2)}, u32[]{:S(2)}) %collective-permute-start.14) | collective-permute-done | bytes 458784 | tf_op jit(solution)/shard_map/ppermute | solution.py:54
  164.3 8.0 %collective-permute-done.18 = bf16[512,448]{0,1:T(8,128)(2,1)S(1)} collective-permute-done((bf16[512,448]{0,1:T(8,128)(2,1)S(1)}, bf16[512,448]{0,1:T(8,128)(2,1)S(1)}, u32[]{:S(2)}, u32[]{:S(2)}) %collective-permute-start.18) | collective-permute-done | bytes 458784 | tf_op jit(solution)/shard_map/ppermute | solution.py:54
  174.1 8.0 %collective-permute-done.22 = bf16[512,448]{0,1:T(8,128)(2,1)S(1)} collective-permute-done((bf16[512,448]{0,1:T(8,128)(2,1)S(1)}, bf16[512,448]{0,1:T(8,128)(2,1)S(1)}, u32[]{:S(2)}, u32[]{:S(2)}) %collective-permute-start.22) | collective-permute-done | bytes 458784 | tf_op jit(solution)/shard_map/ppermute | solution.py:54
  182.2 1.9 fusion.11
  184.1 7.1 %collective-permute-done.26 = bf16[512,448]{0,1:T(8,128)(2,1)S(1)} collective-permute-done((bf16[512,448]{0,1:T(8,128)(2,1)S(1)}, bf16[512,448]{0,1:T(8,128)(2,1)S(1)}, u32[]{:S(2)}, u32[]{:S(2)}) %collective-permute-start.26) | collective-permute-done | bytes 458784 | tf_op jit(solution)/shard_map/ppermute | solution.py:54
  193.0 2.2 %pad_maximum_fusion = f32[2048,448]{0,1:T(8,128)} fusion(f32[512,448]{0,1:T(8,128)S(1)} %fusion.10, f32[512,448]{0,1:T(8,128)S(1)} %fusion.11, f32[512,448]{0,1:T(8,128)S(1)} %fusion.12, f32[512,448]{0,1:T(8,128)S(1)} %fusion.13), kind=kLoop, calls=%fused_computation.10 | loop fusion | flops 2752512 | bytes 7340032 | tf_op jit(solution)/shard_map/concatenate | solution.py:151
  (106 shorter events, 48.9 us)
Async XLA Ops:
  0.7 24.5 %collective-permute-start.1 = (bf16[128,3584]{1,0:T(8,128)(2,1)}, bf16[128,3584]{1,0:T(8,128)(2,1)}, u32[]{:S(2)}, u32[]{:S(2)}) collective-permute-start(bf16[128,3584]{1,0:T(8,128)(2,1)} %param.10), channel_id=1, source_target_pairs={{0,2},{1,3},{2,0},{3,1},{4,6},{5,7},{6,4},{7,5},{8,10},{9,11},{10,... | collective-permute-start | bytes 2752520 | tf_op jit(solution)/shard_map/ppermute | solution.py:51
  3.7 26.2 %collective-permute-start.4 = (bf16[128,1024]{1,0:T(8,128)(2,1)}, bf16[128,1024]{1,0:T(8,128)(2,1)S(1)}, u32[]{:S(2)}, u32[]{:S(2)}) collective-permute-start(bf16[128,1024]{1,0:T(8,128)(2,1)} %param.13), channel_id=1, source_target_pairs={{0,2},{1,3},{2,0},{3,1},{4,6},{5,7},{6,4},{7,5},{8,10},{9,11},{10,... | collective-permute-start | bytes 786440 | tf_op jit(solution)/shard_map/ppermute | solution.py:51
  3.8 26.5 %collective-permute-start.3 = (bf16[128,1024]{1,0:T(8,128)(2,1)}, bf16[128,1024]{1,0:T(8,128)(2,1)S(1)}, u32[]{:S(2)}, u32[]{:S(2)}) collective-permute-start(bf16[128,1024]{1,0:T(8,128)(2,1)} %param.13), channel_id=1, source_target_pairs={{0,1},{1,0},{2,3},{3,2},{4,5},{5,4},{6,7},{7,6},{8,9},{9,8},{10,11... | collective-permute-start | bytes 786440 | tf_op jit(solution)/shard_map/ppermute | solution.py:51
  3.8 34.4 %collective-permute-start = (bf16[128,3584]{1,0:T(8,128)(2,1)}, bf16[128,3584]{1,0:T(8,128)(2,1)}, u32[]{:S(2)}, u32[]{:S(2)}) collective-permute-start(bf16[128,3584]{1,0:T(8,128)(2,1)} %param.10), channel_id=1, source_target_pairs={{0,1},{1,0},{2,3},{3,2},{4,5},{5,4},{6,7},{7,6},{8,9},{9,8},{10,11... | collective-permute-start | bytes 2752520 | tf_op jit(solution)/shard_map/ppermute | solution.py:51
  27.3 33.9 %collective-permute-start.6 = (bf16[256,512]{1,0:T(8,128)(2,1)}, bf16[256,512]{1,0:T(8,128)(2,1)}, u32[]{:S(2)}, u32[]{:S(2)}) collective-permute-start(bf16[256,512]{1,0:T(8,128)(2,1)} %get-tuple-element.8), channel_id=1, source_target_pairs={{0,8},{4,12},{8,16},{12,20},{16,24},{20,28},{24,0},{28,4},{1,9},{5... | collective-permute-start | bytes 786440 | tf_op jit(solution)/shard_map/ppermute | solution.py:58
  30.3 32.1 %collective-permute-start.15 = (bf16[256,512]{1,0:T(8,128)(2,1)}, bf16[256,512]{1,0:T(8,128)(2,1)}, u32[]{:S(2)}, u32[]{:S(2)}) collective-permute-start(bf16[256,512]{1,0:T(8,128)(2,1)} %get-tuple-element.9), channel_id=1, source_target_pairs={{0,8},{4,12},{8,16},{12,20},{16,24},{20,28},{24,0},{28,4},{1,9},{5... | collective-permute-start | bytes 786440 | tf_op jit(solution)/shard_map/ppermute | solution.py:58
  32.1 31.9 %collective-permute-start.19 = (bf16[256,512]{1,0:T(8,128)(2,1)}, bf16[256,512]{1,0:T(8,128)(2,1)}, u32[]{:S(2)}, u32[]{:S(2)}) collective-permute-start(bf16[256,512]{1,0:T(8,128)(2,1)} %get-tuple-element.11), channel_id=1, source_target_pairs={{0,8},{4,12},{8,16},{12,20},{16,24},{20,28},{24,0},{28,4},{1,9},{5... | collective-permute-start | bytes 786440 | tf_op jit(solution)/shard_map/ppermute | solution.py:58
  38.2 27.7 %collective-permute-start.23 = (bf16[256,512]{1,0:T(8,128)(2,1)S(1)}, bf16[256,512]{1,0:T(8,128)(2,1)}, u32[]{:S(2)}, u32[]{:S(2)}) collective-permute-start(bf16[256,512]{1,0:T(8,128)(2,1)S(1)} %get-tuple-element.10), channel_id=1, source_target_pairs={{0,8},{4,12},{8,16},{12,20},{16,24},{20,28},{24,0},{28,4},{1,9},{5... | collective-permute-start | bytes 786440 | tf_op jit(solution)/shard_map/ppermute | solution.py:58
  45.7 48.0 %collective-permute-start.27 = (bf16[4,32,3584]{2,1,0:T(8,128)(2,1)}, bf16[4,32,3584]{2,1,0:T(8,128)(2,1)}, u32[]{:S(2)}, u32[]{:S(2)}) collective-permute-start(bf16[4,32,3584]{2,1,0:T(8,128)(2,1)} %fusion.25), channel_id=1, source_target_pairs={{0,4},{4,0},{8,12},{12,8},{16,20},{20,16},{24,28},{28,24},{1,5},{5... | collective-permute-start | bytes 2752520 | tf_op jit(solution)/shard_map/ppermute | solution.py:54
  62.4 28.0 %collective-permute-start.10 = (bf16[2,64,448]{2,1,0:T(8,128)(2,1)S(1)}, bf16[2,64,448]{2,1,0:T(8,128)(2,1)S(1)}, u32[]{:S(2)}, u32[]{:S(2)}) collective-permute-start(bf16[2,64,448]{2,1,0:T(8,128)(2,1)S(1)} %pad_maximum_fusion.15), channel_id=1, source_target_pairs={{0,16},{4,20},{8,24},{12,28},{16,0},{20,4},{24,8},{28,12},{1,17},{... | collective-permute-start | bytes 344072 | tf_op jit(solution)/shard_map/ppermute | solution.py:58
  64.1 26.3 %collective-permute-start.11 = (bf16[2,64,448]{2,1,0:T(8,128)(2,1)S(1)}, bf16[2,64,448]{2,1,0:T(8,128)(2,1)S(1)}, u32[]{:S(2)}, u32[]{:S(2)}) collective-permute-start(bf16[2,64,448]{2,1,0:T(8,128)(2,1)S(1)} %pad_maximum_fusion.16), channel_id=1, source_target_pairs={{0,24},{4,28},{8,0},{12,4},{16,8},{20,12},{24,16},{28,20},{1,25},{... | collective-permute-start | bytes 344072 | tf_op jit(solution)/shard_map/ppermute | solution.py:58
  65.8 31.8 %collective-permute-start.7 = (bf16[256,512]{1,0:T(8,128)(2,1)}, bf16[256,512]{1,0:T(8,128)(2,1)S(1)}, u32[]{:S(2)}, u32[]{:S(2)}) collective-permute-start(bf16[256,512]{1,0:T(8,128)(2,1)} %collective-permute-done.6), channel_id=1, source_target_pairs={{0,8},{4,12},{8,16},{12,20},{16,24},{20,28},{24,0},{28,4},{1,9},{5... | collective-permute-start | bytes 786440 | tf_op jit(solution)/shard_map/ppermute | solution.py:58
  69.6 28.1 %collective-permute-start.16 = (bf16[256,512]{1,0:T(8,128)(2,1)}, bf16[256,512]{1,0:T(8,128)(2,1)S(1)}, u32[]{:S(2)}, u32[]{:S(2)}) collective-permute-start(bf16[256,512]{1,0:T(8,128)(2,1)} %collective-permute-done.15), channel_id=1, source_target_pairs={{0,8},{4,12},{8,16},{12,20},{16,24},{20,28},{24,0},{28,4},{1,9},{5... | collective-permute-start | bytes 786440 | tf_op jit(solution)/shard_map/ppermute | solution.py:58
  90.4 18.8 %collective-permute-start.20 = (bf16[256,512]{1,0:T(8,128)(2,1)}, bf16[256,512]{1,0:T(8,128)(2,1)}, u32[]{:S(2)}, u32[]{:S(2)}) collective-permute-start(bf16[256,512]{1,0:T(8,128)(2,1)} %collective-permute-done.19), channel_id=1, source_target_pairs={{0,8},{4,12},{8,16},{12,20},{16,24},{20,28},{24,0},{28,4},{1,9},{5... | collective-permute-start | bytes 786440 | tf_op jit(solution)/shard_map/ppermute | solution.py:58
  90.4 20.8 %collective-permute-start.24 = (bf16[256,512]{1,0:T(8,128)(2,1)}, bf16[256,512]{1,0:T(8,128)(2,1)}, u32[]{:S(2)}, u32[]{:S(2)}) collective-permute-start(bf16[256,512]{1,0:T(8,128)(2,1)} %collective-permute-done.23), channel_id=1, source_target_pairs={{0,8},{4,12},{8,16},{12,20},{16,24},{20,28},{24,0},{28,4},{1,9},{5... | collective-permute-start | bytes 786440 | tf_op jit(solution)/shard_map/ppermute | solution.py:58
  97.7 20.5 %collective-permute-start.29 = (bf16[32,3584]{1,0:T(8,128)(2,1)}, bf16[32,3584]{1,0:T(8,128)(2,1)}, u32[]{:S(2)}, u32[]{:S(2)}) collective-permute-start(bf16[32,3584]{1,0:T(8,128)(2,1)} %get-tuple-element.7), channel_id=1, source_target_pairs={{0,16},{4,20},{8,24},{12,28},{16,0},{20,4},{24,8},{28,12},{1,17},{... | collective-permute-start | bytes 688136 | tf_op jit(solution)/shard_map/ppermute | solution.py:58
  107.4 33.9 %collective-permute-start.30 = (bf16[32,3584]{1,0:T(8,128)(2,1)}, bf16[32,3584]{1,0:T(8,128)(2,1)}, u32[]{:S(2)}, u32[]{:S(2)}) collective-permute-start(bf16[32,3584]{1,0:T(8,128)(2,1)} %get-tuple-element.6), channel_id=1, source_target_pairs={{0,24},{4,28},{8,0},{12,4},{16,8},{20,12},{24,16},{28,20},{1,25},{... | collective-permute-start | bytes 688136 | tf_op jit(solution)/shard_map/ppermute | solution.py:58
  109.1 37.3 %collective-permute-start.8 = (bf16[256,512]{1,0:T(8,128)(2,1)}, bf16[256,512]{1,0:T(8,128)(2,1)}, u32[]{:S(2)}, u32[]{:S(2)}) collective-permute-start(bf16[256,512]{1,0:T(8,128)(2,1)} %copy-done.8), channel_id=1, source_target_pairs={{0,8},{4,12},{8,16},{12,20},{16,24},{20,28},{24,0},{28,4},{1,9},{5... | collective-permute-start | bytes 786440 | tf_op jit(solution)/shard_map/ppermute | solution.py:58
  111.2 38.5 %collective-permute-start.17 = (bf16[256,512]{1,0:T(8,128)(2,1)}, bf16[256,512]{1,0:T(8,128)(2,1)}, u32[]{:S(2)}, u32[]{:S(2)}) collective-permute-start(bf16[256,512]{1,0:T(8,128)(2,1)} %copy-done.6), channel_id=1, source_target_pairs={{0,8},{4,12},{8,16},{12,20},{16,24},{20,28},{24,0},{28,4},{1,9},{5... | collective-permute-start | bytes 786440 | tf_op jit(solution)/shard_map/ppermute | solution.py:58
  111.5 41.6 %collective-permute-start.21 = (bf16[256,512]{1,0:T(8,128)(2,1)}, bf16[256,512]{1,0:T(8,128)(2,1)}, u32[]{:S(2)}, u32[]{:S(2)}) collective-permute-start(bf16[256,512]{1,0:T(8,128)(2,1)} %collective-permute-done.20), channel_id=1, source_target_pairs={{0,8},{4,12},{8,16},{12,20},{16,24},{20,28},{24,0},{28,4},{1,9},{5... | collective-permute-start | bytes 786440 | tf_op jit(solution)/shard_map/ppermute | solution.py:58
  118.2 37.3 %collective-permute-start.25 = (bf16[256,512]{1,0:T(8,128)(2,1)}, bf16[256,512]{1,0:T(8,128)(2,1)}, u32[]{:S(2)}, u32[]{:S(2)}) collective-permute-start(bf16[256,512]{1,0:T(8,128)(2,1)} %collective-permute-done.24), channel_id=1, source_target_pairs={{0,8},{4,12},{8,16},{12,20},{16,24},{20,28},{24,0},{28,4},{1,9},{5... | collective-permute-start | bytes 786440 | tf_op jit(solution)/shard_map/ppermute | solution.py:58
  151.5 20.9 %collective-permute-start.18 = (bf16[512,448]{0,1:T(8,128)(2,1)S(1)}, bf16[512,448]{0,1:T(8,128)(2,1)S(1)}, u32[]{:S(2)}, u32[]{:S(2)}) collective-permute-start(bf16[512,448]{0,1:T(8,128)(2,1)S(1)} %fusion.15), channel_id=1, source_target_pairs={{0,4},{4,0},{8,12},{12,8},{16,20},{20,16},{24,28},{28,24},{1,5},{5... | collective-permute-start | bytes 1376264 | tf_op jit(solution)/shard_map/ppermute | solution.py:54
  154.9 27.2 %collective-permute-start.22 = (bf16[512,448]{0,1:T(8,128)(2,1)S(1)}, bf16[512,448]{0,1:T(8,128)(2,1)S(1)}, u32[]{:S(2)}, u32[]{:S(2)}) collective-permute-start(bf16[512,448]{0,1:T(8,128)(2,1)S(1)} %fusion.16), channel_id=1, source_target_pairs={{0,4},{4,0},{8,12},{12,8},{16,20},{20,16},{24,28},{28,24},{1,5},{5... | collective-permute-start | bytes 1376264 | tf_op jit(solution)/shard_map/ppermute | solution.py:54
  157.3 33.9 %collective-permute-start.26 = (bf16[512,448]{0,1:T(8,128)(2,1)S(1)}, bf16[512,448]{0,1:T(8,128)(2,1)S(1)}, u32[]{:S(2)}, u32[]{:S(2)}) collective-permute-start(bf16[512,448]{0,1:T(8,128)(2,1)S(1)} %fusion.17), channel_id=1, source_target_pairs={{0,4},{4,0},{8,12},{12,8},{16,20},{20,16},{24,28},{28,24},{1,5},{5... | collective-permute-start | bytes 1376264 | tf_op jit(solution)/shard_map/ppermute | solution.py:54
  (19 other events, 220.2 us)

commit v2 on v0

v2 whole, which is shorter than its diff:
```python
import math

import jax
import jax.numpy as jnp
from jax import lax
from jax.sharding import PartitionSpec as P

CONTRACT_LAST = (((1,), (1,)), ((), ()))
ROWS_BY_COLS = (((1,), (0,)), ((), ()))
COLS_BY_LAST = (((0,), (1,)), ((), ()))
PARTS = 4
F32 = jnp.float32
BF16 = jnp.bfloat16


def dot(a, b, dims):
    return lax.dot_general(a, b, dims, preferred_element_type=F32)


def strides_of(count):
    found = []
    step = count // 2
    while step:
        found.append(step)
        step //= 2
    return found


def at(array, index, axis=0):
    return lax.dynamic_index_in_dim(array, index, axis, keepdims=False)


def on_device(hidden, connector, routing, talker_in, norm_gain, kv_weight, kv_grad):
    dp_count = lax.axis_size("dp")
    tensor_count = lax.axis_size("tensor")
    pair = 2
    line = dp_count // pair
    rows_dev, width = hidden.shape
    capacity, features = talker_in.shape
    kv_cols = kv_grad.shape[1]
    cols = features // dp_count
    share = cols // tensor_count
    factor = 1.0 / math.sqrt(rows_dev * dp_count)
    dp_pos = lax.axis_index("dp")
    tensor_pos = lax.axis_index("tensor")
    line_pos, pair_pos = dp_pos // pair, dp_pos % pair
    lines = [[i * pair + j for i in range(line)] for j in range(pair)]
    steps = strides_of(tensor_count)

    def tensor_swap(array, step):
        return lax.ppermute(array, "tensor", [(i, i ^ step) for i in range(tensor_count)])

    def pair_swap(array):
        return lax.ppermute(array, "dp", [(i, i ^ 1) for i in range(dp_count)])

    def line_shift(array, by):
        moves = [(i, ((i // pair + by) % line) * pair + i % pair) for i in range(dp_count)]
        return lax.ppermute(array, "dp", moves)

    def digit(step):
        return (tensor_pos // step) % 2

    def tensor_blocks(array, some):
        for step in some:
            array = jnp.concatenate([array, tensor_swap(array, step)], axis=-1)
        return array

    def tensor_split(array, some):
        for step in some:
            own, other = at(array, digit(step), array.ndim - 3), at(array, 1 - digit(step), array.ndim - 3)
            array = jnp.concatenate([own, tensor_swap(other, step)], axis=-1)
        return array

    def tensor_gather(array, axis, some):
        for step in some:
            other = tensor_swap(array, step)
            array = jnp.where(
                digit(step) == 0,
                jnp.stack([array, other], axis=axis),
                jnp.stack([other, array], axis=axis),
            )
        return array

    def line_exchange(blocks):
        return lax.all_to_all(
            blocks, "dp", split_axis=0, concat_axis=0, tiled=True, axis_index_groups=lines
        )

    together = lax.optimization_barrier
    far_step, near_steps = steps[:1], steps[1:]
    twos = (2,) * len(steps)

    held = lax.all_gather(hidden, "dp", axis=0, tiled=True, axis_index_groups=lines)

    routes = routing[:, 0]
    row_ids = jnp.arange(rows_dev)
    same = routes[:, None] == routes[None, :]
    ranks = jnp.sum((same & (row_ids[None, :] < row_ids[:, None])).astype(jnp.int32), axis=1)
    distance = routes ^ tensor_pos
    place = jnp.zeros_like(routes)
    for k, step in enumerate(steps):
        place = place + ((distance // step) % 2) * (1 << k)
    spot = place * capacity + ranks
    pick = (spot[:, None] == jnp.arange(tensor_count * capacity)[None, :]).astype(BF16)

    inputs = talker_in.T.astype(F32)
    inv_rms = lax.rsqrt(jnp.mean(inputs * inputs, axis=0, keepdims=True) + 1e-06)
    scaled = inputs * inv_rms
    gain = norm_gain[:, None]
    gain_back = gain * dot(kv_weight, kv_grad, CONTRACT_LAST)
    grad = (
        inv_rms * (gain_back - scaled * jnp.mean(gain_back * scaled, axis=0, keepdims=True))
    ).astype(BF16)
    normed = (scaled * gain).astype(BF16).reshape(twos + (features // tensor_count, capacity))

    shares = tensor_split(grad.reshape((dp_count,) + twos + (share, capacity)), far_step)
    shares = tensor_split(shares, near_steps)
    rows = dot(shares.reshape(dp_count * share, -1), pick, CONTRACT_LAST).astype(BF16)
    rows, normed, kv_t = together((rows.reshape(dp_count, share, rows_dev), normed, kv_grad.T))
    normed = tensor_split(normed, far_step)
    kv_slots = tensor_blocks(kv_t, far_step)

    sided = rows.reshape(line, 2, share, rows_dev)
    sided = jnp.where(pair_pos == 0, sided, sided[:, ::-1])
    got = [at(sided, line_pos)]
    got += [line_shift(at(sided, (line_pos + s) % line), s) for s in range(1, line)]
    normed = dot(tensor_split(normed, near_steps), pick, CONTRACT_LAST).astype(BF16)
    masked = dot(tensor_blocks(kv_slots, near_steps), pick, CONTRACT_LAST).astype(BF16)
    per_dev = kv_cols // (dp_count * tensor_count)
    block = kv_cols // dp_count
    masked = masked.reshape(line, 2, block, rows_dev)
    own = at(masked, pair_pos, 1).reshape(line * block, rows_dev)
    other = at(masked, 1 - pair_pos, 1).reshape(line * block, rows_dev)
    row_grad = tensor_gather(rows, 1, far_step)
    got, row_grad, own, normed, sent = together(
        (got, row_grad, own, normed, jnp.concatenate([other, normed], axis=0))
    )
    origin = (line_pos - jnp.arange(line)) % line
    got = jnp.take(jnp.stack(got), origin, axis=0)
    got = got.transpose(1, 2, 0, 3).reshape(2, share, line * rows_dev)
    got = tensor_gather(got, 1, far_step)
    far = pair_swap(sent)
    grads = tensor_gather(got, 1, near_steps).reshape(2, cols, line * rows_dev)
    row_grad = tensor_gather(row_grad, 1, near_steps).reshape(features, rows_dev)
    terms = dot(own, normed, CONTRACT_LAST)
    terms = terms + dot(far[:line * block], far[line * block:], CONTRACT_LAST)
    terms = (terms * factor).reshape(line, block, -1)
    held, grads, row_grad, terms = together((held, grads, row_grad, terms))

    part = width // PARTS
    held = [held[:, c * part:(c + 1) * part] for c in range(PARTS)]
    fars = [(dot(grads[1], rows, ROWS_BY_COLS) * factor).astype(BF16) for rows in held]
    gots = [pair_swap(far) for far in fars]
    terms, row_grad, fars[-1] = together((terms, row_grad, fars[-1]))
    hidden_grad = dot(row_grad, connector, COLS_BY_LAST).astype(BF16)
    kv_out = at(terms, line_pos)
    for s in range(1, line):
        kv_out = kv_out + line_shift(at(terms, (line_pos + s) % line).astype(BF16), s).astype(F32)
    kv_out = kv_out.reshape(twos + (per_dev, -1))
    for k, step in enumerate(steps):
        own, other = at(kv_out, digit(step)), at(kv_out, 1 - digit(step))
        other = tensor_swap(other, step)
        spot = len(steps) - k
        kv_out = jnp.where(
            digit(step) == 0,
            jnp.stack([own, other], axis=spot),
            jnp.stack([other, own], axis=spot),
        )
    kv_weight_grad = kv_out.reshape(per_dev, features).T
    gots[1], hidden_grad = together((gots[1], hidden_grad))
    outs = [
        dot(rows, grads[0], COLS_BY_LAST) * factor + got.T.astype(F32)
        for rows, got in zip(held, gots)
    ]
    connector_grad = jnp.concatenate(outs, axis=0)
    return (hidden_grad, connector_grad, kv_weight_grad)


def solution(mesh):
    return jax.shard_map(
        on_device,
        mesh=mesh,
        in_specs=(
            P("dp", "tensor"),
            P("tensor", None),
            P("dp", None),
            P(("dp", "tensor"), None),
            P(),
            P(),
            P(("dp", "tensor"), None),
        ),
        out_specs=(P("dp", "tensor"), P("tensor", "dp"), P(None, ("dp", "tensor"))),
        check_vma=False,
    )
```

time: 650 us -> 166 us (0.26)
  waiting for transfers between devices: 578 us -> 67.8 us
  starting transfers between devices: 0.34 us -> 28.3 us
  blocking collectives: 10.1 us -> 0 us
    reduce_scatter x2 -> x0, waiting for transfers between devices: 526 us -> none  [the longest x1 468 us: on_device(): lax.psum_scatter(conn_terms, 'dp', scatter_dimension=1, tiled=True)]
    ppermute x0 -> x23, waiting for transfers between devices: none -> 59.4 us  [the longest x12 39.8 us: tensor_swap(): lax.ppermute(array, 'tensor', [(i, i ^ step) for i in range(tensor_count)])]
    all_gather x2 -> x1, waiting for transfers between devices: 51.3 us -> 7.76 us  [on_device(): lax.all_gather(hidden, 'dp', axis=0, tiled=True, axis_index_groups=lines)]
    ppermute x0 -> x23, starting transfers between devices: none -> 28.3 us  [the longest x6 12.1 us: line_shift(): return lax.ppermute(array, 'dp', moves)]
    all_to_all x1 -> x0, blocking collectives: 10.1 us -> none  [on_device(): lax.all_to_all(regrouped, 'tensor', split_axis=1, concat_axis=0, tiled=True)]
    dot_general x4 -> x15, matrix products: 31.6 us -> 33.7 us  [dot(): return lax.dot_general(a, b, dims, preferred_element_type=F32)]
  transfers between devices with their start and end apart: 4 -> 24, of which waited for: 4 -> 13; matrix products, arithmetic and copies ran while one was open for 5% -> 27% of each run, Pallas kernels for 0% -> 0%
where the time goes in v2:
time: 166 us
  waiting for transfers between devices  67.8 us (41%)
  matrix products  33.7 us (20%)
  starting transfers between devices  28.3 us (17%)
  between operations  14.6 us (9%)
  other arithmetic  12.8 us (8%)
  local copies, waits for them, and re-layouts  8.82 us (5%)
    ppermute x12, waiting for transfers between devices, tensor_swap(): lax.ppermute(array, 'tensor', [(i, i ^ step) for i in range(tensor_count)])  39.8 us
    dot_general x15, matrix products, dot(): return lax.dot_general(a, b, dims, preferred_element_type=F32)  33.7 us
    ppermute x5, waiting for transfers between devices, pair_swap(): return lax.ppermute(array, 'dp', [(i, i ^ 1) for i in range(dp_count)])  16.9 us
    ppermute x6, starting transfers between devices, line_shift(): return lax.ppermute(array, 'dp', moves)  12.1 us
    ppermute x12, starting transfers between devices, tensor_swap(): lax.ppermute(array, 'tensor', [(i, i ^ step) for i in range(tensor_count)])  10.5 us
    all_gather x1, waiting for transfers between devices, on_device(): lax.all_gather(hidden, 'dp', axis=0, tiled=True, axis_index_groups=lines)  7.76 us
    ppermute x5, starting transfers between devices, pair_swap(): return lax.ppermute(array, 'dp', [(i, i ^ 1) for i in range(dp_count)])  5.65 us
    select_n x5, other arithmetic, tensor_gather(): jnp.where(digit(step) == 0, jnp.stack([array, other], axis=axis), jnp.sta...  3.63 us
  transfers between devices with their start and end apart: 24, of which 13 were waited for; matrix products, arithmetic and copies ran while one was open for 27% of the time, Pallas kernels for 0%

profile of v2, /device:TPU:0, one launch (start us, length us, event | category | flops | bytes accessed | tf_op | source)
XLA Modules:
  0.0 165.9 jit_solution(14912875916640314533)
XLA Ops:
  10.0 6.4 %fusion.5 = (f32[128]{0:T(128)S(1)}, f32[3584,128]{1,0:T(8,128)}) fusion(bf16[128,3584]{0,1:T(8,128)(2,1)S(1)} %copy.19, f32[128]{0:T(128)S(1)} %add_rsqrt_fusion, bf16[3584,1024]{1,0:T(8,128)(2,1)} %param.12, bf16[128,1024]{1,0:T(8,128)(2,1)S(1)} %copy-done.2, f32[3584]{0:T(1024)S(1)} %copy-done.5), kind=kOutput, calls=%fused_computation.11 | convolution fusion | flops 941817728 | bytes 10370048 | tf_op jit(solution)/shard_map/dot_general | solution.py:17
  16.4 2.7 %fusion.9 = (bf16[3584,128]{1,0:T(8,128)(2,1)S(1)}, bf16[3584,128]{1,0:T(8,128)(2,1)S(1)}) fusion(bf16[128,3584]{0,1:T(8,128)(2,1)S(1)} %copy.19, f32[128]{0:T(128)S(1)} %add_rsqrt_fusion, f32[3584]{0:T(1024)S(1)} %copy-done.5, f32[3584,128]{1,0:T(8,128)} %get-tuple-element.67, f32[128]{0:T(128)S(1)} %broadcast_multiply_fusion), kind=kLoop, calls=%fused_computation.15 | loop fusion | flops 3670016 | bytes 4602880 | tf_op jit(solution)/shard_map/convert_element_type | solution.py:114
  19.3 3.1 %collective-permute-start = (bf16[8,2,112,128]{3,2,1,0:T(8,128)(2,1)S(1)}, bf16[8,2,112,128]{3,2,1,0:T(8,128)(2,1)S(1)}, u32[]{:S(2)}, u32[]{:S(2)}) collective-permute-start(bf16[8,2,112,128]{3,2,1,0:T(8,128)(2,1)S(1)} %get-tuple-element.52), channel_id=1, source_target_pairs={{0,2},{1,3},{2,0},{3,1},{4,6},{5,7},{6,4},{7,5},{8,10},{9,11},{10,... | collective-permute-start | bytes 1376264 | tf_op jit(solution)/shard_map/ppermute | solution.py:51
  22.3 10.5 %collective-permute-done = bf16[8,2,112,128]{3,2,1,0:T(8,128)(2,1)S(1)} collective-permute-done((bf16[8,2,112,128]{3,2,1,0:T(8,128)(2,1)S(1)}, bf16[8,2,112,128]{3,2,1,0:T(8,128)(2,1)S(1)}, u32[]{:S(2)}, u32[]{:S(2)}) %collective-permute-start) | collective-permute-done | bytes 458784 | tf_op jit(solution)/shard_map/ppermute | solution.py:51
  39.4 5.1 %collective-permute-done.6 = bf16[1024,128]{0,1:T(8,128)(2,1)S(1)} collective-permute-done((bf16[1024,128]{0,1:T(8,128)(2,1)S(1)}, bf16[1024,128]{0,1:T(8,128)(2,1)S(1)}, u32[]{:S(2)}, u32[]{:S(2)}) %collective-permute-start.6) | collective-permute-done | bytes 262176 | tf_op jit(solution)/shard_map/ppermute | solution.py:51
  46.7 2.6 %collective-permute-start.3 = (bf16[2,112,256]{2,1,0:T(8,128)(2,1)S(1)}, bf16[2,112,256]{2,1,0:T(8,128)(2,1)S(1)}, u32[]{:S(2)}, u32[]{:S(2)}) collective-permute-start(bf16[2,112,256]{2,1,0:T(8,128)(2,1)S(1)} %get-tuple-element.63), channel_id=1, source_target_pairs={{0,16},{4,20},{8,24},{12,28},{16,0},{20,4},{24,8},{28,12},{1,17},{... | collective-permute-start | bytes 344072 | tf_op jit(solution)/shard_map/ppermute | solution.py:58
  49.2 5.1 %collective-permute-done.8 = bf16[2,896,128]{2,1,0:T(8,128)(2,1)S(1)} collective-permute-done((bf16[2,896,128]{2,1,0:T(8,128)(2,1)S(1)}, bf16[2,896,128]{2,1,0:T(8,128)(2,1)S(1)}, u32[]{:S(2)}, u32[]{:S(2)}) %collective-permute-start.8) | collective-permute-done | bytes 458784 | tf_op jit(solution)/shard_map/ppermute | solution.py:51
  54.4 3.8 %collective-permute-start.4 = (bf16[2,112,256]{2,1,0:T(8,128)(2,1)S(1)}, bf16[2,112,256]{2,1,0:T(8,128)(2,1)S(1)}, u32[]{:S(2)}, u32[]{:S(2)}) collective-permute-start(bf16[2,112,256]{2,1,0:T(8,128)(2,1)S(1)} %get-tuple-element.62), channel_id=1, source_target_pairs={{0,24},{4,28},{8,0},{12,4},{16,8},{20,12},{24,16},{28,20},{1,25},{... | collective-permute-start | bytes 344072 | tf_op jit(solution)/shard_map/ppermute | solution.py:58
  58.3 5.1 %collective-permute-done.5 = bf16[8,112,256]{2,1,0:T(8,128)(2,1)S(1)} collective-permute-done((bf16[8,112,256]{2,1,0:T(8,128)(2,1)S(1)}, bf16[8,112,256]{2,1,0:T(8,128)(2,1)S(1)}, u32[]{:S(2)}, u32[]{:S(2)}) %collective-permute-start.5) | collective-permute-done | bytes 458784 | tf_op jit(solution)/shard_map/ppermute | solution.py:51
  72.5 8.5 %collective-permute-done.10 = bf16[2,112,1024]{2,1,0:T(8,128)(2,1)S(1)} collective-permute-done((bf16[2,112,1024]{2,1,0:T(8,128)(2,1)}, bf16[2,112,1024]{2,1,0:T(8,128)(2,1)S(1)}, u32[]{:S(2)}, u32[]{:S(2)}) %collective-permute-start.10) | collective-permute-done | bytes 458784 | tf_op jit(solution)/shard_map/ppermute | solution.py:51
  81.5 6.8 %collective-permute-done.13 = bf16[1408,256]{1,0:T(8,128)(2,1)} collective-permute-done((bf16[1408,256]{1,0:T(8,128)(2,1)}, bf16[1408,256]{1,0:T(8,128)(2,1)}, u32[]{:S(2)}, u32[]{:S(2)}) %collective-permute-start.13) | collective-permute-done | bytes 720928 | tf_op jit(solution)/shard_map/ppermute | solution.py:54
  90.3 2.9 %maximum_select_fusion.1 = bf16[8,2,2,112,256]{4,3,2,1,0:T(8,128)(2,1)} fusion(bf16[8,1,2,112,256]{4,3,2,1,0:T(8,128)(2,1)} %bitcast.38, bf16[8,1,2,112,256]{4,3,2,1,0:T(8,128)(2,1)S(1)} %bitcast.139, pred[]{:T(512)S(6)} %eq.74), kind=kLoop, calls=%fused_computation.17 | loop fusion | flops 2752512 | bytes 3670017 | tf_op jit(solution)/shard_map/jit(_where)/select_n | solution.py:77
  95.0 7.8 %all-gather.2.cloned.1.call-done = bf16[1024,2048]{1,0:T(8,128)(2,1)} async-done(((bf16[256,2048]{1,0:T(8,128)(2,1)}), bf16[1024,2048]{1,0:T(8,128)(2,1)}) %all-gather.2.cloned.1.call-update) | async-done | bytes 4194320 | tf_op jit(solution)/shard_map/all_gather | solution.py:93
  102.7 3.0 %fusion.11 = bf16[448,512]{1,0:T(8,128)(2,1)} fusion(bf16[1024,2048]{1,0:T(8,128)(2,1)} %all-gather.2.cloned.1.call-done, bf16[2,448,1024]{2,1,0:T(8,128)(2,1)} %bitcast.140), kind=kOutput, calls=%fused_computation.29 | convolution fusion | flops 470220800 | bytes 2424832 | tf_op jit(solution)/shard_map/dot_general | solution.py:17
  105.8 2.7 %fusion.12 = bf16[448,512]{1,0:T(8,128)(2,1)} fusion(bf16[1024,2048]{1,0:T(8,128)(2,1)} %all-gather.2.cloned.1.call-done, bf16[2,448,1024]{2,1,0:T(8,128)(2,1)S(1)} %bitcast.141), kind=kOutput, calls=%fused_computation.30 | convolution fusion | flops 470220800 | bytes 2424832 | tf_op jit(solution)/shard_map/dot_general | solution.py:17
  108.4 2.8 %fusion.10 = bf16[448,512]{1,0:T(8,128)(2,1)} fusion(bf16[1024,2048]{1,0:T(8,128)(2,1)} %all-gather.2.cloned.1.call-done, bf16[2,448,1024]{2,1,0:T(8,128)(2,1)S(1)} %bitcast.142), kind=kOutput, calls=%fused_computation.28 | convolution fusion | flops 470220800 | bytes 2424832 | tf_op jit(solution)/shard_map/dot_general | solution.py:17
  114.9 2.4 %collective-permute-start.20 = (bf16[128,896]{1,0:T(8,128)(2,1)S(1)}, bf16[128,896]{1,0:T(8,128)(2,1)}, u32[]{:S(2)}, u32[]{:S(2)}) collective-permute-start(bf16[128,896]{1,0:T(8,128)(2,1)S(1)} %get-tuple-element.42), channel_id=1, source_target_pairs={{0,24},{4,28},{8,0},{12,4},{16,8},{20,12},{24,16},{28,20},{1,25},{... | collective-permute-start | bytes 688136 | tf_op jit(solution)/shard_map/ppermute | solution.py:58
  117.8 8.5 %convolution_convert_fusion = bf16[256,2048]{1,0:T(8,128)(2,1)} fusion(bf16[3584,256]{1,0:T(8,128)(2,1)S(1)} %bitcast.148, bf16[2048,3584]{1,0:T(8,128)(2,1)} %param.8), kind=kOutput, calls=%fused_computation.3 | convolution fusion | flops 3758620672 | bytes 17563648 | tf_op jit(solution)/shard_map/dot_general | solution.py:17
  126.3 2.0 %fusion.13 = bf16[448,512]{1,0:T(8,128)(2,1)S(1)} fusion(bf16[1024,2048]{1,0:T(8,128)(2,1)} %all-gather.2.cloned.1.call-done, bf16[2,448,1024]{2,1,0:T(8,128)(2,1)S(1)} %bitcast.143), kind=kOutput, calls=%fused_computation.31 | convolution fusion | flops 470220800 | bytes 2424832 | tf_op jit(solution)/shard_map/dot_general | solution.py:17
  129.9 2.6 %collective-permute-done.19 = bf16[128,896]{1,0:T(8,128)(2,1)S(1)} collective-permute-done((bf16[128,896]{1,0:T(8,128)(2,1)S(1)}, bf16[128,896]{1,0:T(8,128)(2,1)S(1)}, u32[]{:S(2)}, u32[]{:S(2)}) %collective-permute-start.19) | collective-permute-done | bytes 229408 | tf_op jit(solution)/shard_map/ppermute | solution.py:58
  136.6 3.7 %collective-permute-done.21 = f32[2,32,896]{2,1,0:T(8,128)S(1)} collective-permute-done((f32[2,32,896]{2,1,0:T(8,128)S(1)}, f32[2,32,896]{2,1,0:T(8,128)S(1)}, u32[]{:S(2)}, u32[]{:S(2)}) %collective-permute-start.21) | collective-permute-done | bytes 229408 | tf_op jit(solution)/shard_map/ppermute | solution.py:51
  141.3 3.2 %collective-permute-done.14 = bf16[448,512]{1,0:T(8,128)(2,1)S(1)} collective-permute-done((bf16[448,512]{1,0:T(8,128)(2,1)}, bf16[448,512]{1,0:T(8,128)(2,1)S(1)}, u32[]{:S(2)}, u32[]{:S(2)}) %collective-permute-start.14) | collective-permute-done | bytes 458784 | tf_op jit(solution)/shard_map/ppermute | solution.py:54
  146.3 6.9 %collective-permute-done.16 = bf16[448,512]{1,0:T(8,128)(2,1)S(1)} collective-permute-done((bf16[448,512]{1,0:T(8,128)(2,1)S(1)}, bf16[448,512]{1,0:T(8,128)(2,1)S(1)}, u32[]{:S(2)}, u32[]{:S(2)}) %collective-permute-start.16) | collective-permute-done | bytes 458784 | tf_op jit(solution)/shard_map/ppermute | solution.py:54
  155.5 2.2 %pad_maximum_fusion = f32[2048,448]{0,1:T(8,128)} fusion(f32[512,448]{0,1:T(8,128)S(1)} %bitcast_add_fusion, f32[512,448]{0,1:T(8,128)S(1)} %bitcast_add_fusion.1, f32[512,448]{0,1:T(8,128)S(1)} %bitcast_add_fusion.2, f32[512,448]{0,1:T(8,128)S(1)} %bitcast_add_fusion.3), kind=kLoop, calls=%fused_computation.2 | loop fusion | flops 2752512 | bytes 7340032 | tf_op jit(solution)/shard_map/concatenate | solution.py:175
  (99 shorter events, 40.9 us)
Async XLA Ops:
  7.2 95.6 %all-gather.2.cloned.1.call-start = ((), (), s32[]{:S(2)}) async-start(), calls=%async_computation | async-start | bytes 5242880 | tf_op jit(solution)/shard_map/all_gather | solution.py:93
  19.3 13.6 %collective-permute-start = (bf16[8,2,112,128]{3,2,1,0:T(8,128)(2,1)S(1)}, bf16[8,2,112,128]{3,2,1,0:T(8,128)(2,1)S(1)}, u32[]{:S(2)}, u32[]{:S(2)}) collective-permute-start(bf16[8,2,112,128]{3,2,1,0:T(8,128)(2,1)S(1)} %get-tuple-element.52), channel_id=1, source_target_pairs={{0,2},{1,3},{2,0},{3,1},{4,6},{5,7},{6,4},{7,5},{8,10},{9,11},{10,... | collective-permute-start | bytes 1376264 | tf_op jit(solution)/shard_map/ppermute | solution.py:51
  32.9 1.9 %collective-permute-start.1 = (bf16[8,112,256]{2,1,0:T(8,128)(2,1)S(1)}, bf16[8,112,256]{2,1,0:T(8,128)(2,1)S(1)}, u32[]{:S(2)}, u32[]{:S(2)}) collective-permute-start(bf16[8,112,256]{2,1,0:T(8,128)(2,1)S(1)} %get-tuple-element.51), channel_id=1, source_target_pairs={{0,1},{1,0},{2,3},{3,2},{4,5},{5,4},{6,7},{7,6},{8,9},{9,8},{10,11... | collective-permute-start | bytes 1376264 | tf_op jit(solution)/shard_map/ppermute | solution.py:51
  35.3 9.2 %collective-permute-start.6 = (bf16[1024,128]{0,1:T(8,128)(2,1)S(1)}, bf16[1024,128]{0,1:T(8,128)(2,1)S(1)}, u32[]{:S(2)}, u32[]{:S(2)}) collective-permute-start(bf16[1024,128]{0,1:T(8,128)(2,1)S(1)} %bitcast.163), channel_id=1, source_target_pairs={{0,2},{1,3},{2,0},{3,1},{4,6},{5,7},{6,4},{7,5},{8,10},{9,11},{10,... | collective-permute-start | bytes 786440 | tf_op jit(solution)/shard_map/ppermute | solution.py:51
  37.3 17.0 %collective-permute-start.8 = (bf16[2,896,128]{2,1,0:T(8,128)(2,1)S(1)}, bf16[2,896,128]{2,1,0:T(8,128)(2,1)S(1)}, u32[]{:S(2)}, u32[]{:S(2)}) collective-permute-start(bf16[2,896,128]{2,1,0:T(8,128)(2,1)S(1)} %get-tuple-element.48), channel_id=1, source_target_pairs={{0,2},{1,3},{2,0},{3,1},{4,6},{5,7},{6,4},{7,5},{8,10},{9,11},{10,... | collective-permute-start | bytes 1376264 | tf_op jit(solution)/shard_map/ppermute | solution.py:51
  37.7 25.7 %collective-permute-start.5 = (bf16[8,112,256]{2,1,0:T(8,128)(2,1)S(1)}, bf16[8,112,256]{2,1,0:T(8,128)(2,1)S(1)}, u32[]{:S(2)}, u32[]{:S(2)}) collective-permute-start(bf16[8,112,256]{2,1,0:T(8,128)(2,1)S(1)} %bitcast.149), channel_id=1, source_target_pairs={{0,2},{1,3},{2,0},{3,1},{4,6},{5,7},{6,4},{7,5},{8,10},{9,11},{10,... | collective-permute-start | bytes 1376264 | tf_op jit(solution)/shard_map/ppermute | solution.py:51
  44.6 18.9 %collective-permute-start.7 = (bf16[1024,256]{0,1:T(8,128)(2,1)S(1)}, bf16[1024,256]{0,1:T(8,128)(2,1)S(1)}, u32[]{:S(2)}, u32[]{:S(2)}) collective-permute-start(bf16[1024,256]{0,1:T(8,128)(2,1)S(1)} %pad_maximum_fusion.2), channel_id=1, source_target_pairs={{0,1},{1,0},{2,3},{3,2},{4,5},{5,4},{6,7},{7,6},{8,9},{9,8},{10,11... | collective-permute-start | bytes 1572872 | tf_op jit(solution)/shard_map/ppermute | solution.py:51
  44.8 21.9 %collective-permute-start.2 = (bf16[2,112,256]{2,1,0:T(8,128)(2,1)S(1)}, bf16[2,112,256]{2,1,0:T(8,128)(2,1)S(1)}, u32[]{:S(2)}, u32[]{:S(2)}) collective-permute-start(bf16[2,112,256]{2,1,0:T(8,128)(2,1)S(1)} %get-tuple-element.64), channel_id=1, source_target_pairs={{0,8},{4,12},{8,16},{12,20},{16,24},{20,28},{24,0},{28,4},{1,9},{5... | collective-permute-start | bytes 344072 | tf_op jit(solution)/shard_map/ppermute | solution.py:58
  46.7 20.0 %collective-permute-start.3 = (bf16[2,112,256]{2,1,0:T(8,128)(2,1)S(1)}, bf16[2,112,256]{2,1,0:T(8,128)(2,1)S(1)}, u32[]{:S(2)}, u32[]{:S(2)}) collective-permute-start(bf16[2,112,256]{2,1,0:T(8,128)(2,1)S(1)} %get-tuple-element.63), channel_id=1, source_target_pairs={{0,16},{4,20},{8,24},{12,28},{16,0},{20,4},{24,8},{28,12},{1,17},{... | collective-permute-start | bytes 344072 | tf_op jit(solution)/shard_map/ppermute | solution.py:58
  54.4 12.3 %collective-permute-start.4 = (bf16[2,112,256]{2,1,0:T(8,128)(2,1)S(1)}, bf16[2,112,256]{2,1,0:T(8,128)(2,1)S(1)}, u32[]{:S(2)}, u32[]{:S(2)}) collective-permute-start(bf16[2,112,256]{2,1,0:T(8,128)(2,1)S(1)} %get-tuple-element.62), channel_id=1, source_target_pairs={{0,24},{4,28},{8,0},{12,4},{16,8},{20,12},{24,16},{28,20},{1,25},{... | collective-permute-start | bytes 344072 | tf_op jit(solution)/shard_map/ppermute | solution.py:58
  63.4 1.8 %collective-permute-start.9 = (bf16[896,256]{1,0:T(8,128)(2,1)S(1)}, bf16[896,256]{1,0:T(8,128)(2,1)S(1)}, u32[]{:S(2)}, u32[]{:S(2)}) collective-permute-start(bf16[896,256]{1,0:T(8,128)(2,1)S(1)} %get-tuple-element.47), channel_id=1, source_target_pairs={{0,1},{1,0},{2,3},{3,2},{4,5},{5,4},{6,7},{7,6},{8,9},{9,8},{10,11... | collective-permute-start | bytes 1376264 | tf_op jit(solution)/shard_map/ppermute | solution.py:51
  68.3 12.8 %collective-permute-start.10 = (bf16[2,112,1024]{2,1,0:T(8,128)(2,1)}, bf16[2,112,1024]{2,1,0:T(8,128)(2,1)S(1)}, u32[]{:S(2)}, u32[]{:S(2)}) collective-permute-start(bf16[2,112,1024]{2,1,0:T(8,128)(2,1)} %bitcast.58), channel_id=1, source_target_pairs={{0,2},{1,3},{2,0},{3,1},{4,6},{5,7},{6,4},{7,5},{8,10},{9,11},{10,... | collective-permute-start | bytes 1376264 | tf_op jit(solution)/shard_map/ppermute | solution.py:51
  70.0 18.2 %collective-permute-start.13 = (bf16[1408,256]{1,0:T(8,128)(2,1)}, bf16[1408,256]{1,0:T(8,128)(2,1)}, u32[]{:S(2)}, u32[]{:S(2)}) collective-permute-start(bf16[1408,256]{1,0:T(8,128)(2,1)} %pad_maximum_fusion.1), channel_id=1, source_target_pairs={{0,4},{4,0},{8,12},{12,8},{16,20},{20,16},{24,28},{28,24},{1,5},{5... | collective-permute-start | bytes 2162696 | tf_op jit(solution)/shard_map/ppermute | solution.py:54
  71.5 18.8 %collective-permute-start.12 = (bf16[8,2,112,256]{3,2,1,0:T(8,128)(2,1)S(1)}, bf16[8,2,112,256]{3,2,1,0:T(8,128)(2,1)}, u32[]{:S(2)}, u32[]{:S(2)}) collective-permute-start(bf16[8,2,112,256]{3,2,1,0:T(8,128)(2,1)S(1)} %maximum_select_fusion.2), channel_id=1, source_target_pairs={{0,1},{1,0},{2,3},{3,2},{4,5},{5,4},{6,7},{7,6},{8,9},{9,8},{10,11... | collective-permute-start | bytes 2752520 | tf_op jit(solution)/shard_map/ppermute | solution.py:51
  81.2 12.0 %collective-permute-start.11 = (bf16[2,2,112,1024]{3,2,0,1:T(8,128)(2,1)S(1)}, bf16[2,2,112,1024]{3,2,0,1:T(8,128)(2,1)S(1)}, u32[]{:S(2)}, u32[]{:S(2)}) collective-permute-start(bf16[2,2,112,1024]{3,2,0,1:T(8,128)(2,1)S(1)} %maximum_select_fusion.4), channel_id=1, source_target_pairs={{0,1},{1,0},{2,3},{3,2},{4,5},{5,4},{6,7},{7,6},{8,9},{9,8},{10,11... | collective-permute-start | bytes 2752520 | tf_op jit(solution)/shard_map/ppermute | solution.py:51
  111.2 42.6 %collective-permute-start.17 = (bf16[448,512]{1,0:T(8,128)(2,1)}, bf16[448,512]{1,0:T(8,128)(2,1)}, u32[]{:S(2)}, u32[]{:S(2)}) collective-permute-start(bf16[448,512]{1,0:T(8,128)(2,1)} %fusion.11), channel_id=1, source_target_pairs={{0,4},{4,0},{8,12},{12,8},{16,20},{20,16},{24,28},{28,24},{1,5},{5... | collective-permute-start | bytes 1376264 | tf_op jit(solution)/shard_map/ppermute | solution.py:54
  113.5 14.8 %collective-permute-start.18 = (bf16[128,896]{1,0:T(8,128)(2,1)}, bf16[128,896]{1,0:T(8,128)(2,1)S(1)}, u32[]{:S(2)}, u32[]{:S(2)}) collective-permute-start(bf16[128,896]{1,0:T(8,128)(2,1)} %get-tuple-element.41), channel_id=1, source_target_pairs={{0,8},{4,12},{8,16},{12,20},{16,24},{20,28},{24,0},{28,4},{1,9},{5... | collective-permute-start | bytes 688136 | tf_op jit(solution)/shard_map/ppermute | solution.py:58
  113.5 19.1 %collective-permute-start.19 = (bf16[128,896]{1,0:T(8,128)(2,1)S(1)}, bf16[128,896]{1,0:T(8,128)(2,1)S(1)}, u32[]{:S(2)}, u32[]{:S(2)}) collective-permute-start(bf16[128,896]{1,0:T(8,128)(2,1)S(1)} %get-tuple-element.43), channel_id=1, source_target_pairs={{0,16},{4,20},{8,24},{12,28},{16,0},{20,4},{24,8},{28,12},{1,17},{... | collective-permute-start | bytes 688136 | tf_op jit(solution)/shard_map/ppermute | solution.py:58
  114.9 18.2 %collective-permute-start.20 = (bf16[128,896]{1,0:T(8,128)(2,1)S(1)}, bf16[128,896]{1,0:T(8,128)(2,1)}, u32[]{:S(2)}, u32[]{:S(2)}) collective-permute-start(bf16[128,896]{1,0:T(8,128)(2,1)S(1)} %get-tuple-element.42), channel_id=1, source_target_pairs={{0,24},{4,28},{8,0},{12,4},{16,8},{20,12},{24,16},{28,20},{1,25},{... | collective-permute-start | bytes 688136 | tf_op jit(solution)/shard_map/ppermute | solution.py:58
  117.3 27.2 %collective-permute-start.15 = (bf16[448,512]{1,0:T(8,128)(2,1)}, bf16[448,512]{1,0:T(8,128)(2,1)}, u32[]{:S(2)}, u32[]{:S(2)}) collective-permute-start(bf16[448,512]{1,0:T(8,128)(2,1)} %fusion.12), channel_id=1, source_target_pairs={{0,4},{4,0},{8,12},{12,8},{16,20},{20,16},{24,28},{28,24},{1,5},{5... | collective-permute-start | bytes 1376264 | tf_op jit(solution)/shard_map/ppermute | solution.py:54
  128.4 16.1 %collective-permute-start.14 = (bf16[448,512]{1,0:T(8,128)(2,1)}, bf16[448,512]{1,0:T(8,128)(2,1)S(1)}, u32[]{:S(2)}, u32[]{:S(2)}) collective-permute-start(bf16[448,512]{1,0:T(8,128)(2,1)} %fusion.10), channel_id=1, source_target_pairs={{0,4},{4,0},{8,12},{12,8},{16,20},{20,16},{24,28},{28,24},{1,5},{5... | collective-permute-start | bytes 1376264 | tf_op jit(solution)/shard_map/ppermute | solution.py:54
  132.6 20.6 %collective-permute-start.16 = (bf16[448,512]{1,0:T(8,128)(2,1)S(1)}, bf16[448,512]{1,0:T(8,128)(2,1)S(1)}, u32[]{:S(2)}, u32[]{:S(2)}) collective-permute-start(bf16[448,512]{1,0:T(8,128)(2,1)S(1)} %fusion.13), channel_id=1, source_target_pairs={{0,4},{4,0},{8,12},{12,8},{16,20},{20,16},{24,28},{28,24},{1,5},{5... | collective-permute-start | bytes 1376264 | tf_op jit(solution)/shard_map/ppermute | solution.py:54
  134.2 6.1 %collective-permute-start.21 = (f32[2,32,896]{2,1,0:T(8,128)S(1)}, f32[2,32,896]{2,1,0:T(8,128)S(1)}, u32[]{:S(2)}, u32[]{:S(2)}) collective-permute-start(f32[2,32,896]{2,1,0:T(8,128)S(1)} %get-tuple-element.61), channel_id=1, source_target_pairs={{0,2},{1,3},{2,0},{3,1},{4,6},{5,7},{6,4},{7,5},{8,10},{9,11},{10,... | collective-permute-start | bytes 688136 | tf_op jit(solution)/shard_map/ppermute | solution.py:51
  141.2 16.5 %collective-permute-start.22 = (f32[32,2,896]{2,1,0:T(2,128)S(1)}, f32[32,2,896]{2,1,0:T(2,128)S(1)}, u32[]{:S(2)}, u32[]{:S(2)}) collective-permute-start(f32[32,2,896]{2,1,0:T(2,128)S(1)} %get-tuple-element.59), channel_id=1, source_target_pairs={{0,1},{1,0},{2,3},{3,2},{4,5},{5,4},{6,7},{7,6},{8,9},{9,8},{10,11... | collective-permute-start | bytes 688136 | tf_op jit(solution)/shard_map/ppermute | solution.py:51
  (8 other events, 56.2 us)
Sparse Core Ops, SparseCore 0:
  9.6 93.1 all-gather.1

commit v3 on v2

--- a/solution.py
+++ b/solution.py
@@ -148,11 +148,17 @@
     held, grads, row_grad, terms = together((held, grads, row_grad, terms))
 
     part = width // PARTS
-    held = [held[:, c * part:(c + 1) * part] for c in range(PARTS)]
-    fars = [(dot(grads[1], rows, ROWS_BY_COLS) * factor).astype(BF16) for rows in held]
-    gots = [pair_swap(far) for far in fars]
-    terms, row_grad, fars[-1] = together((terms, row_grad, fars[-1]))
+    gots, blocks = [], []
+    for c in range(PARTS):
+        if c > 1:
+            gots[c - 2], held = together((gots[c - 2], held))
+        blocks.append(held[:, c * part:(c + 1) * part])
+        far_c = (dot(grads[1], blocks[c], ROWS_BY_COLS) * factor).astype(BF16)
+        if c == 2:
+            far_c, row_grad = together((far_c, row_grad))
+        gots.append(pair_swap(far_c))
     hidden_grad = dot(row_grad, connector, COLS_BY_LAST).astype(BF16)
+    gots[0], terms = together((gots[0], terms))
     kv_out = at(terms, line_pos)
     for s in range(1, line):
         kv_out = kv_out + line_shift(at(terms, (line_pos + s) % line).astype(BF16), s).astype(F32)
@@ -167,10 +173,10 @@
             jnp.stack([other, own], axis=spot),
         )
     kv_weight_grad = kv_out.reshape(per_dev, features).T
-    gots[1], hidden_grad = together((gots[1], hidden_grad))
+    gots[2], hidden_grad = together((gots[2], hidden_grad))
     outs = [
         dot(rows, grads[0], COLS_BY_LAST) * factor + got.T.astype(F32)
-        for rows, got in zip(held, gots)
+        for rows, got in zip(blocks, gots)
     ]
     connector_grad = jnp.concatenate(outs, axis=0)
     return (hidden_grad, connector_grad, kv_weight_grad)

time: 166 us -> 164 us (0.988)
    ppermute x6, waiting for transfers between devices: 2.63 us -> 0.02 us  [line_shift(): return lax.ppermute(array, 'dp', moves)]
  transfers between devices with their start and end apart: 24 -> 24, of which waited for: 13 -> 12; matrix products, arithmetic and copies ran while one was open for 27% -> 31% of each run, Pallas kernels for 0% -> 0%
where the time goes in v3:
time: 164 us; the launch traced here: 163 us
  waiting for transfers between devices  66.8 us (41%)
  matrix products  32.5 us (20%)
  starting transfers between devices  28.3 us (17%)
  between operations  14.6 us (9%)
  other arithmetic  12.9 us (8%)
  local copies, waits for them, and re-layouts  8.16 us (5%)
    ppermute x12, waiting for transfers between devices, tensor_swap(): lax.ppermute(array, 'tensor', [(i, i ^ step) for i in range(tensor_count)])  41.2 us
    dot_general x15, matrix products, dot(): return lax.dot_general(a, b, dims, preferred_element_type=F32)  32.5 us
    ppermute x5, waiting for transfers between devices, pair_swap(): return lax.ppermute(array, 'dp', [(i, i ^ 1) for i in range(dp_count)])  17.1 us
    ppermute x6, starting transfers between devices, line_shift(): return lax.ppermute(array, 'dp', moves)  12.1 us
    ppermute x12, starting transfers between devices, tensor_swap(): lax.ppermute(array, 'tensor', [(i, i ^ step) for i in range(tensor_count)])  10.5 us
    all_gather x1, waiting for transfers between devices, on_device(): lax.all_gather(hidden, 'dp', axis=0, tiled=True, axis_index_groups=lines)  7.77 us
    ppermute x5, starting transfers between devices, pair_swap(): return lax.ppermute(array, 'dp', [(i, i ^ 1) for i in range(dp_count)])  5.67 us
    select_n x5, other arithmetic, tensor_gather(): jnp.where(digit(step) == 0, jnp.stack([array, other], axis=axis), jnp.sta...  3.63 us
  transfers between devices with their start and end apart: 24, of which 12 were waited for; matrix products, arithmetic and copies ran while one was open for 31% of the time, Pallas kernels for 0%

profile of v3, /device:TPU:0, one launch (start us, length us, event | category | flops | bytes accessed | tf_op | source)
XLA Modules:
  0.0 163.3 jit_solution(13560752862716389073)
XLA Ops:
  10.0 6.4 %fusion.5 = (f32[128]{0:T(128)S(1)}, f32[3584,128]{1,0:T(8,128)}) fusion(bf16[128,3584]{0,1:T(8,128)(2,1)S(1)} %copy.19, f32[128]{0:T(128)S(1)} %add_rsqrt_fusion, bf16[3584,1024]{1,0:T(8,128)(2,1)} %param.12, bf16[128,1024]{1,0:T(8,128)(2,1)S(1)} %copy-done.3, f32[3584]{0:T(1024)S(1)} %copy-done.4), kind=kOutput, calls=%fused_computation.11 | convolution fusion | flops 941817728 | bytes 10370048 | tf_op jit(solution)/shard_map/dot_general | solution.py:17
  16.4 2.7 %fusion.9 = (bf16[3584,128]{1,0:T(8,128)(2,1)S(1)}, bf16[3584,128]{1,0:T(8,128)(2,1)S(1)}) fusion(bf16[128,3584]{0,1:T(8,128)(2,1)S(1)} %copy.19, f32[128]{0:T(128)S(1)} %add_rsqrt_fusion, f32[3584]{0:T(1024)S(1)} %copy-done.4, f32[3584,128]{1,0:T(8,128)} %get-tuple-element.79, f32[128]{0:T(128)S(1)} %broadcast_multiply_fusion), kind=kLoop, calls=%fused_computation.15 | loop fusion | flops 3670016 | bytes 4602880 | tf_op jit(solution)/shard_map/convert_element_type | solution.py:114
  19.3 3.1 %collective-permute-start = (bf16[8,2,112,128]{3,2,1,0:T(8,128)(2,1)S(1)}, bf16[8,2,112,128]{3,2,1,0:T(8,128)(2,1)S(1)}, u32[]{:S(2)}, u32[]{:S(2)}) collective-permute-start(bf16[8,2,112,128]{3,2,1,0:T(8,128)(2,1)S(1)} %get-tuple-element.64), channel_id=1, source_target_pairs={{0,2},{1,3},{2,0},{3,1},{4,6},{5,7},{6,4},{7,5},{8,10},{9,11},{10,... | collective-permute-start | bytes 1376264 | tf_op jit(solution)/shard_map/ppermute | solution.py:51
  22.3 10.5 %collective-permute-done = bf16[8,2,112,128]{3,2,1,0:T(8,128)(2,1)S(1)} collective-permute-done((bf16[8,2,112,128]{3,2,1,0:T(8,128)(2,1)S(1)}, bf16[8,2,112,128]{3,2,1,0:T(8,128)(2,1)S(1)}, u32[]{:S(2)}, u32[]{:S(2)}) %collective-permute-start) | collective-permute-done | bytes 458784 | tf_op jit(solution)/shard_map/ppermute | solution.py:51
  35.3 1.8 %collective-permute-start.6 = (bf16[1024,128]{0,1:T(8,128)(2,1)S(1)}, bf16[1024,128]{0,1:T(8,128)(2,1)S(1)}, u32[]{:S(2)}, u32[]{:S(2)}) collective-permute-start(bf16[1024,128]{0,1:T(8,128)(2,1)S(1)} %bitcast.157), channel_id=1, source_target_pairs={{0,2},{1,3},{2,0},{3,1},{4,6},{5,7},{6,4},{7,5},{8,10},{9,11},{10,... | collective-permute-start | bytes 786440 | tf_op jit(solution)/shard_map/ppermute | solution.py:51
  39.4 5.1 %collective-permute-done.6 = bf16[1024,128]{0,1:T(8,128)(2,1)S(1)} collective-permute-done((bf16[1024,128]{0,1:T(8,128)(2,1)S(1)}, bf16[1024,128]{0,1:T(8,128)(2,1)S(1)}, u32[]{:S(2)}, u32[]{:S(2)}) %collective-permute-start.6) | collective-permute-done | bytes 262176 | tf_op jit(solution)/shard_map/ppermute | solution.py:51
  44.8 1.8 %collective-permute-start.2 = (bf16[2,112,256]{2,1,0:T(8,128)(2,1)S(1)}, bf16[2,112,256]{2,1,0:T(8,128)(2,1)S(1)}, u32[]{:S(2)}, u32[]{:S(2)}) collective-permute-start(bf16[2,112,256]{2,1,0:T(8,128)(2,1)S(1)} %get-tuple-element.76), channel_id=1, source_target_pairs={{0,8},{4,12},{8,16},{12,20},{16,24},{20,28},{24,0},{28,4},{1,9},{5... | collective-permute-start | bytes 344072 | tf_op jit(solution)/shard_map/ppermute | solution.py:58
  46.7 2.6 %collective-permute-start.3 = (bf16[2,112,256]{2,1,0:T(8,128)(2,1)S(1)}, bf16[2,112,256]{2,1,0:T(8,128)(2,1)S(1)}, u32[]{:S(2)}, u32[]{:S(2)}) collective-permute-start(bf16[2,112,256]{2,1,0:T(8,128)(2,1)S(1)} %get-tuple-element.75), channel_id=1, source_target_pairs={{0,16},{4,20},{8,24},{12,28},{16,0},{20,4},{24,8},{28,12},{1,17},{... | collective-permute-start | bytes 344072 | tf_op jit(solution)/shard_map/ppermute | solution.py:58
  49.3 5.1 %collective-permute-done.8 = bf16[2,896,128]{2,1,0:T(8,128)(2,1)S(1)} collective-permute-done((bf16[2,896,128]{2,1,0:T(8,128)(2,1)S(1)}, bf16[2,896,128]{2,1,0:T(8,128)(2,1)S(1)}, u32[]{:S(2)}, u32[]{:S(2)}) %collective-permute-start.8) | collective-permute-done | bytes 458784 | tf_op jit(solution)/shard_map/ppermute | solution.py:51
  54.4 3.8 %collective-permute-start.4 = (bf16[2,112,256]{2,1,0:T(8,128)(2,1)S(1)}, bf16[2,112,256]{2,1,0:T(8,128)(2,1)S(1)}, u32[]{:S(2)}, u32[]{:S(2)}) collective-permute-start(bf16[2,112,256]{2,1,0:T(8,128)(2,1)S(1)} %get-tuple-element.74), channel_id=1, source_target_pairs={{0,24},{4,28},{8,0},{12,4},{16,8},{20,12},{24,16},{28,20},{1,25},{... | collective-permute-start | bytes 344072 | tf_op jit(solution)/shard_map/ppermute | solution.py:58
  58.3 5.1 %collective-permute-done.5 = bf16[8,112,256]{2,1,0:T(8,128)(2,1)S(1)} collective-permute-done((bf16[8,112,256]{2,1,0:T(8,128)(2,1)S(1)}, bf16[8,112,256]{2,1,0:T(8,128)(2,1)S(1)}, u32[]{:S(2)}, u32[]{:S(2)}) %collective-permute-start.5) | collective-permute-done | bytes 458784 | tf_op jit(solution)/shard_map/ppermute | solution.py:51
  72.5 8.5 %collective-permute-done.10 = bf16[2,112,1024]{2,1,0:T(8,128)(2,1)S(1)} collective-permute-done((bf16[2,112,1024]{2,1,0:T(8,128)(2,1)}, bf16[2,112,1024]{2,1,0:T(8,128)(2,1)S(1)}, u32[]{:S(2)}, u32[]{:S(2)}) %collective-permute-start.10) | collective-permute-done | bytes 458784 | tf_op jit(solution)/shard_map/ppermute | solution.py:51
  81.5 6.8 %collective-permute-done.13 = bf16[1408,256]{1,0:T(8,128)(2,1)} collective-permute-done((bf16[1408,256]{1,0:T(8,128)(2,1)}, bf16[1408,256]{1,0:T(8,128)(2,1)}, u32[]{:S(2)}, u32[]{:S(2)}) %collective-permute-start.13) | collective-permute-done | bytes 720928 | tf_op jit(solution)/shard_map/ppermute | solution.py:54
  90.3 2.9 %maximum_select_fusion.1 = bf16[8,2,2,112,256]{4,3,2,1,0:T(8,128)(2,1)} fusion(bf16[8,1,2,112,256]{4,3,2,1,0:T(8,128)(2,1)} %bitcast.38, bf16[8,1,2,112,256]{4,3,2,1,0:T(8,128)(2,1)S(1)} %bitcast.133, pred[]{:T(512)S(6)} %eq.74), kind=kLoop, calls=%fused_computation.17 | loop fusion | flops 2752512 | bytes 3670017 | tf_op jit(solution)/shard_map/jit(_where)/select_n | solution.py:77
  95.0 7.8 %all-gather.2.cloned.1.call-done = bf16[1024,2048]{1,0:T(8,128)(2,1)} async-done(((bf16[256,2048]{1,0:T(8,128)(2,1)}), bf16[1024,2048]{1,0:T(8,128)(2,1)}) %all-gather.2.cloned.1.call-update) | async-done | bytes 4194320 | tf_op jit(solution)/shard_map/all_gather | solution.py:93
  102.7 2.3 %fusion.13 = bf16[448,512]{1,0:T(8,128)(2,1)S(1)} fusion(bf16[1024,2048]{1,0:T(8,128)(2,1)} %all-gather.2.cloned.1.call-done, bf16[2,448,1024]{2,1,0:T(8,128)(2,1)} %bitcast.134), kind=kOutput, calls=%fused_computation.31 | convolution fusion | flops 470220800 | bytes 2424832 | tf_op jit(solution)/shard_map/dot_general | solution.py:17
  106.6 1.9 %fusion.15 = bf16[448,512]{1,0:T(8,128)(2,1)S(1)} fusion(bf16[1024,2048]{1,0:T(8,128)(2,1)} %all-gather.2.cloned.1.call-done, bf16[2,448,1024]{2,1,0:T(8,128)(2,1)S(1)} %bitcast.135), kind=kOutput, calls=%fused_computation.33 | convolution fusion | flops 470220800 | bytes 2424832 | tf_op jit(solution)/shard_map/dot_general | solution.py:17
  110.7 7.8 %collective-permute-done.14 = bf16[448,512]{1,0:T(8,128)(2,1)S(1)} collective-permute-done((bf16[448,512]{1,0:T(8,128)(2,1)S(1)}, bf16[448,512]{1,0:T(8,128)(2,1)S(1)}, u32[]{:S(2)}, u32[]{:S(2)}) %collective-permute-start.14) | collective-permute-done | bytes 458784 | tf_op jit(solution)/shard_map/ppermute | solution.py:54
  120.7 2.6 %collective-permute-start.20 = (bf16[128,896]{1,0:T(8,128)(2,1)S(1)}, bf16[128,896]{1,0:T(8,128)(2,1)}, u32[]{:S(2)}, u32[]{:S(2)}) collective-permute-start(bf16[128,896]{1,0:T(8,128)(2,1)S(1)} %get-tuple-element.54), channel_id=1, source_target_pairs={{0,24},{4,28},{8,0},{12,4},{16,8},{20,12},{24,16},{28,20},{1,25},{... | collective-permute-start | bytes 688136 | tf_op jit(solution)/shard_map/ppermute | solution.py:58
  124.7 2.5 %collective-permute-done.16 = bf16[448,512]{1,0:T(8,128)(2,1)S(1)} collective-permute-done((bf16[448,512]{1,0:T(8,128)(2,1)S(1)}, bf16[448,512]{1,0:T(8,128)(2,1)S(1)}, u32[]{:S(2)}, u32[]{:S(2)}) %collective-permute-start.16) | collective-permute-done | bytes 458784 | tf_op jit(solution)/shard_map/ppermute | solution.py:54
  130.7 8.5 %convolution_convert_fusion = bf16[256,2048]{1,0:T(8,128)(2,1)} fusion(bf16[3584,256]{1,0:T(8,128)(2,1)S(1)} %bitcast.142, bf16[2048,3584]{1,0:T(8,128)(2,1)} %param.8), kind=kOutput, calls=%fused_computation.3 | convolution fusion | flops 3758620672 | bytes 17563648 | tf_op jit(solution)/shard_map/dot_general | solution.py:17
  139.2 2.0 %fusion.12 = f32[512,448]{0,1:T(8,128)S(1)} fusion(bf16[1024,2048]{1,0:T(8,128)(2,1)} %all-gather.2.cloned.1.call-done, bf16[448,512]{1,0:T(8,128)(2,1)} %copy-done.8, bf16[2,448,1024]{2,1,0:T(8,128)(2,1)S(1)} %bitcast.139), kind=kOutput, calls=%fused_computation.25 | convolution fusion | flops 470450176 | bytes 3342336 | tf_op jit(solution)/shard_map/dot_general | solution.py:17
  144.3 4.2 %collective-permute-done.21 = f32[2,32,896]{2,1,0:T(8,128)S(1)} collective-permute-done((f32[2,32,896]{2,1,0:T(8,128)S(1)}, f32[2,32,896]{2,1,0:T(8,128)S(1)}, u32[]{:S(2)}, u32[]{:S(2)}) %collective-permute-start.21) | collective-permute-done | bytes 229408 | tf_op jit(solution)/shard_map/ppermute | solution.py:51
  152.9 2.1 %pad_maximum_fusion = f32[2048,448]{0,1:T(8,128)} fusion(f32[512,448]{0,1:T(8,128)S(1)} %fusion.10, f32[512,448]{0,1:T(8,128)S(1)} %fusion.11, f32[512,448]{0,1:T(8,128)S(1)} %bitcast_add_fusion, f32[512,448]{0,1:T(8,128)S(1)} %fusion.12), kind=kLoop, calls=%fused_computation.2 | loop fusion | flops 2752512 | bytes 7340032 | tf_op jit(solution)/shard_map/concatenate | solution.py:181
  (101 shorter events, 40.7 us)
Async XLA Ops:
  7.2 95.6 %all-gather.2.cloned.1.call-start = ((), (), s32[]{:S(2)}) async-start(), calls=%async_computation | async-start | bytes 5242880 | tf_op jit(solution)/shard_map/all_gather | solution.py:93
  19.3 13.6 %collective-permute-start = (bf16[8,2,112,128]{3,2,1,0:T(8,128)(2,1)S(1)}, bf16[8,2,112,128]{3,2,1,0:T(8,128)(2,1)S(1)}, u32[]{:S(2)}, u32[]{:S(2)}) collective-permute-start(bf16[8,2,112,128]{3,2,1,0:T(8,128)(2,1)S(1)} %get-tuple-element.64), channel_id=1, source_target_pairs={{0,2},{1,3},{2,0},{3,1},{4,6},{5,7},{6,4},{7,5},{8,10},{9,11},{10,... | collective-permute-start | bytes 1376264 | tf_op jit(solution)/shard_map/ppermute | solution.py:51
  32.9 1.9 %collective-permute-start.1 = (bf16[8,112,256]{2,1,0:T(8,128)(2,1)S(1)}, bf16[8,112,256]{2,1,0:T(8,128)(2,1)S(1)}, u32[]{:S(2)}, u32[]{:S(2)}) collective-permute-start(bf16[8,112,256]{2,1,0:T(8,128)(2,1)S(1)} %get-tuple-element.63), channel_id=1, source_target_pairs={{0,1},{1,0},{2,3},{3,2},{4,5},{5,4},{6,7},{7,6},{8,9},{9,8},{10,11... | collective-permute-start | bytes 1376264 | tf_op jit(solution)/shard_map/ppermute | solution.py:51
  35.3 9.2 %collective-permute-start.6 = (bf16[1024,128]{0,1:T(8,128)(2,1)S(1)}, bf16[1024,128]{0,1:T(8,128)(2,1)S(1)}, u32[]{:S(2)}, u32[]{:S(2)}) collective-permute-start(bf16[1024,128]{0,1:T(8,128)(2,1)S(1)} %bitcast.157), channel_id=1, source_target_pairs={{0,2},{1,3},{2,0},{3,1},{4,6},{5,7},{6,4},{7,5},{8,10},{9,11},{10,... | collective-permute-start | bytes 786440 | tf_op jit(solution)/shard_map/ppermute | solution.py:51
  37.3 17.0 %collective-permute-start.8 = (bf16[2,896,128]{2,1,0:T(8,128)(2,1)S(1)}, bf16[2,896,128]{2,1,0:T(8,128)(2,1)S(1)}, u32[]{:S(2)}, u32[]{:S(2)}) collective-permute-start(bf16[2,896,128]{2,1,0:T(8,128)(2,1)S(1)} %get-tuple-element.60), channel_id=1, source_target_pairs={{0,2},{1,3},{2,0},{3,1},{4,6},{5,7},{6,4},{7,5},{8,10},{9,11},{10,... | collective-permute-start | bytes 1376264 | tf_op jit(solution)/shard_map/ppermute | solution.py:51
  37.7 25.7 %collective-permute-start.5 = (bf16[8,112,256]{2,1,0:T(8,128)(2,1)S(1)}, bf16[8,112,256]{2,1,0:T(8,128)(2,1)S(1)}, u32[]{:S(2)}, u32[]{:S(2)}) collective-permute-start(bf16[8,112,256]{2,1,0:T(8,128)(2,1)S(1)} %bitcast.143), channel_id=1, source_target_pairs={{0,2},{1,3},{2,0},{3,1},{4,6},{5,7},{6,4},{7,5},{8,10},{9,11},{10,... | collective-permute-start | bytes 1376264 | tf_op jit(solution)/shard_map/ppermute | solution.py:51
  44.6 18.9 %collective-permute-start.7 = (bf16[1024,256]{0,1:T(8,128)(2,1)S(1)}, bf16[1024,256]{0,1:T(8,128)(2,1)S(1)}, u32[]{:S(2)}, u32[]{:S(2)}) collective-permute-start(bf16[1024,256]{0,1:T(8,128)(2,1)S(1)} %pad_maximum_fusion.2), channel_id=1, source_target_pairs={{0,1},{1,0},{2,3},{3,2},{4,5},{5,4},{6,7},{7,6},{8,9},{9,8},{10,11... | collective-permute-start | bytes 1572872 | tf_op jit(solution)/shard_map/ppermute | solution.py:51
  44.8 21.8 %collective-permute-start.2 = (bf16[2,112,256]{2,1,0:T(8,128)(2,1)S(1)}, bf16[2,112,256]{2,1,0:T(8,128)(2,1)S(1)}, u32[]{:S(2)}, u32[]{:S(2)}) collective-permute-start(bf16[2,112,256]{2,1,0:T(8,128)(2,1)S(1)} %get-tuple-element.76), channel_id=1, source_target_pairs={{0,8},{4,12},{8,16},{12,20},{16,24},{20,28},{24,0},{28,4},{1,9},{5... | collective-permute-start | bytes 344072 | tf_op jit(solution)/shard_map/ppermute | solution.py:58
  46.7 20.0 %collective-permute-start.3 = (bf16[2,112,256]{2,1,0:T(8,128)(2,1)S(1)}, bf16[2,112,256]{2,1,0:T(8,128)(2,1)S(1)}, u32[]{:S(2)}, u32[]{:S(2)}) collective-permute-start(bf16[2,112,256]{2,1,0:T(8,128)(2,1)S(1)} %get-tuple-element.75), channel_id=1, source_target_pairs={{0,16},{4,20},{8,24},{12,28},{16,0},{20,4},{24,8},{28,12},{1,17},{... | collective-permute-start | bytes 344072 | tf_op jit(solution)/shard_map/ppermute | solution.py:58
  54.4 12.3 %collective-permute-start.4 = (bf16[2,112,256]{2,1,0:T(8,128)(2,1)S(1)}, bf16[2,112,256]{2,1,0:T(8,128)(2,1)S(1)}, u32[]{:S(2)}, u32[]{:S(2)}) collective-permute-start(bf16[2,112,256]{2,1,0:T(8,128)(2,1)S(1)} %get-tuple-element.74), channel_id=1, source_target_pairs={{0,24},{4,28},{8,0},{12,4},{16,8},{20,12},{24,16},{28,20},{1,25},{... | collective-permute-start | bytes 344072 | tf_op jit(solution)/shard_map/ppermute | solution.py:58
  63.4 1.8 %collective-permute-start.9 = (bf16[896,256]{1,0:T(8,128)(2,1)S(1)}, bf16[896,256]{1,0:T(8,128)(2,1)S(1)}, u32[]{:S(2)}, u32[]{:S(2)}) collective-permute-start(bf16[896,256]{1,0:T(8,128)(2,1)S(1)} %get-tuple-element.59), channel_id=1, source_target_pairs={{0,1},{1,0},{2,3},{3,2},{4,5},{5,4},{6,7},{7,6},{8,9},{9,8},{10,11... | collective-permute-start | bytes 1376264 | tf_op jit(solution)/shard_map/ppermute | solution.py:51
  68.3 12.8 %collective-permute-start.10 = (bf16[2,112,1024]{2,1,0:T(8,128)(2,1)}, bf16[2,112,1024]{2,1,0:T(8,128)(2,1)S(1)}, u32[]{:S(2)}, u32[]{:S(2)}) collective-permute-start(bf16[2,112,1024]{2,1,0:T(8,128)(2,1)} %bitcast.58), channel_id=1, source_target_pairs={{0,2},{1,3},{2,0},{3,1},{4,6},{5,7},{6,4},{7,5},{8,10},{9,11},{10,... | collective-permute-start | bytes 1376264 | tf_op jit(solution)/shard_map/ppermute | solution.py:51
  70.0 18.2 %collective-permute-start.13 = (bf16[1408,256]{1,0:T(8,128)(2,1)}, bf16[1408,256]{1,0:T(8,128)(2,1)}, u32[]{:S(2)}, u32[]{:S(2)}) collective-permute-start(bf16[1408,256]{1,0:T(8,128)(2,1)} %pad_maximum_fusion.1), channel_id=1, source_target_pairs={{0,4},{4,0},{8,12},{12,8},{16,20},{20,16},{24,28},{28,24},{1,5},{5... | collective-permute-start | bytes 2162696 | tf_op jit(solution)/shard_map/ppermute | solution.py:54
  71.5 18.8 %collective-permute-start.12 = (bf16[8,2,112,256]{3,2,1,0:T(8,128)(2,1)S(1)}, bf16[8,2,112,256]{3,2,1,0:T(8,128)(2,1)}, u32[]{:S(2)}, u32[]{:S(2)}) collective-permute-start(bf16[8,2,112,256]{3,2,1,0:T(8,128)(2,1)S(1)} %maximum_select_fusion.2), channel_id=1, source_target_pairs={{0,1},{1,0},{2,3},{3,2},{4,5},{5,4},{6,7},{7,6},{8,9},{9,8},{10,11... | collective-permute-start | bytes 2752520 | tf_op jit(solution)/shard_map/ppermute | solution.py:51
  81.2 12.0 %collective-permute-start.11 = (bf16[2,2,112,1024]{3,2,0,1:T(8,128)(2,1)S(1)}, bf16[2,2,112,1024]{3,2,0,1:T(8,128)(2,1)S(1)}, u32[]{:S(2)}, u32[]{:S(2)}) collective-permute-start(bf16[2,2,112,1024]{3,2,0,1:T(8,128)(2,1)S(1)} %maximum_select_fusion.4), channel_id=1, source_target_pairs={{0,1},{1,0},{2,3},{3,2},{4,5},{5,4},{6,7},{7,6},{8,9},{9,8},{10,11... | collective-permute-start | bytes 2752520 | tf_op jit(solution)/shard_map/ppermute | solution.py:51
  105.0 13.5 %collective-permute-start.14 = (bf16[448,512]{1,0:T(8,128)(2,1)S(1)}, bf16[448,512]{1,0:T(8,128)(2,1)S(1)}, u32[]{:S(2)}, u32[]{:S(2)}) collective-permute-start(bf16[448,512]{1,0:T(8,128)(2,1)S(1)} %fusion.13), channel_id=1, source_target_pairs={{0,4},{4,0},{8,12},{12,8},{16,20},{20,16},{24,28},{28,24},{1,5},{5... | collective-permute-start | bytes 1376264 | tf_op jit(solution)/shard_map/ppermute | solution.py:54
  108.5 18.7 %collective-permute-start.16 = (bf16[448,512]{1,0:T(8,128)(2,1)S(1)}, bf16[448,512]{1,0:T(8,128)(2,1)S(1)}, u32[]{:S(2)}, u32[]{:S(2)}) collective-permute-start(bf16[448,512]{1,0:T(8,128)(2,1)S(1)} %fusion.15), channel_id=1, source_target_pairs={{0,4},{4,0},{8,12},{12,8},{16,20},{20,16},{24,28},{28,24},{1,5},{5... | collective-permute-start | bytes 1376264 | tf_op jit(solution)/shard_map/ppermute | solution.py:54
  119.5 21.7 %collective-permute-start.18 = (bf16[128,896]{1,0:T(8,128)(2,1)}, bf16[128,896]{1,0:T(8,128)(2,1)S(1)}, u32[]{:S(2)}, u32[]{:S(2)}) collective-permute-start(bf16[128,896]{1,0:T(8,128)(2,1)} %get-tuple-element.53), channel_id=1, source_target_pairs={{0,8},{4,12},{8,16},{12,20},{16,24},{20,28},{24,0},{28,4},{1,9},{5... | collective-permute-start | bytes 688136 | tf_op jit(solution)/shard_map/ppermute | solution.py:58
  119.5 21.7 %collective-permute-start.19 = (bf16[128,896]{1,0:T(8,128)(2,1)}, bf16[128,896]{1,0:T(8,128)(2,1)}, u32[]{:S(2)}, u32[]{:S(2)}) collective-permute-start(bf16[128,896]{1,0:T(8,128)(2,1)} %get-tuple-element.55), channel_id=1, source_target_pairs={{0,16},{4,20},{8,24},{12,28},{16,0},{20,4},{24,8},{28,12},{1,17},{... | collective-permute-start | bytes 688136 | tf_op jit(solution)/shard_map/ppermute | solution.py:58
  120.7 20.5 %collective-permute-start.20 = (bf16[128,896]{1,0:T(8,128)(2,1)S(1)}, bf16[128,896]{1,0:T(8,128)(2,1)}, u32[]{:S(2)}, u32[]{:S(2)}) collective-permute-start(bf16[128,896]{1,0:T(8,128)(2,1)S(1)} %get-tuple-element.54), channel_id=1, source_target_pairs={{0,24},{4,28},{8,0},{12,4},{16,8},{20,12},{24,16},{28,20},{1,25},{... | collective-permute-start | bytes 688136 | tf_op jit(solution)/shard_map/ppermute | solution.py:58
  127.2 22.3 %collective-permute-start.15 = (bf16[448,512]{1,0:T(8,128)(2,1)}, bf16[448,512]{1,0:T(8,128)(2,1)}, u32[]{:S(2)}, u32[]{:S(2)}) collective-permute-start(bf16[448,512]{1,0:T(8,128)(2,1)} %fusion.14), channel_id=1, source_target_pairs={{0,4},{4,0},{8,12},{12,8},{16,20},{20,16},{24,28},{28,24},{1,5},{5... | collective-permute-start | bytes 1376264 | tf_op jit(solution)/shard_map/ppermute | solution.py:54
  130.1 21.1 %collective-permute-start.17 = (bf16[448,512]{1,0:T(8,128)(2,1)}, bf16[448,512]{1,0:T(8,128)(2,1)}, u32[]{:S(2)}, u32[]{:S(2)}) collective-permute-start(bf16[448,512]{1,0:T(8,128)(2,1)} %fusion.16), channel_id=1, source_target_pairs={{0,4},{4,0},{8,12},{12,8},{16,20},{20,16},{24,28},{28,24},{1,5},{5... | collective-permute-start | bytes 1376264 | tf_op jit(solution)/shard_map/ppermute | solution.py:54
  142.5 6.1 %collective-permute-start.21 = (f32[2,32,896]{2,1,0:T(8,128)S(1)}, f32[2,32,896]{2,1,0:T(8,128)S(1)}, u32[]{:S(2)}, u32[]{:S(2)}) collective-permute-start(f32[2,32,896]{2,1,0:T(8,128)S(1)} %get-tuple-element.73), channel_id=1, source_target_pairs={{0,2},{1,3},{2,0},{3,1},{4,6},{5,7},{6,4},{7,5},{8,10},{9,11},{10,... | collective-permute-start | bytes 688136 | tf_op jit(solution)/shard_map/ppermute | solution.py:51
  149.4 5.6 %collective-permute-start.22 = (f32[32,2,896]{2,1,0:T(2,128)S(1)}, f32[32,2,896]{2,1,0:T(2,128)S(1)}, u32[]{:S(2)}, u32[]{:S(2)}) collective-permute-start(f32[32,2,896]{2,1,0:T(2,128)S(1)} %get-tuple-element.71), channel_id=1, source_target_pairs={{0,1},{1,0},{2,3},{3,2},{4,5},{5,4},{6,7},{7,6},{8,9},{9,8},{10,11... | collective-permute-start | bytes 688136 | tf_op jit(solution)/shard_map/ppermute | solution.py:51
  (9 other events, 48.9 us)
Sparse Core Ops, SparseCore 0:
  9.6 93.1 all-gather.1

commit v4 on v2

--- a/solution.py
+++ b/solution.py
@@ -9,6 +9,7 @@
 ROWS_BY_COLS = (((1,), (0,)), ((), ()))
 COLS_BY_LAST = (((0,), (1,)), ((), ()))
 PARTS = 4
+EARLY = 2
 F32 = jnp.float32
 BF16 = jnp.bfloat16
 
@@ -53,8 +54,8 @@
     def pair_swap(array):
         return lax.ppermute(array, "dp", [(i, i ^ 1) for i in range(dp_count)])
 
-    def line_shift(array, by):
-        moves = [(i, ((i // pair + by) % line) * pair + i % pair) for i in range(dp_count)]
+    def line_swap(array, by):
+        moves = [(i, (i // pair ^ by) * pair + i % pair) for i in range(dp_count)]
         return lax.ppermute(array, "dp", moves)
 
     def digit(step):
@@ -81,16 +82,20 @@
             )
         return array
 
-    def line_exchange(blocks):
-        return lax.all_to_all(
-            blocks, "dp", split_axis=0, concat_axis=0, tiled=True, axis_index_groups=lines
-        )
-
     together = lax.optimization_barrier
     far_step, near_steps = steps[:1], steps[1:]
     twos = (2,) * len(steps)
 
-    held = lax.all_gather(hidden, "dp", axis=0, tiled=True, axis_index_groups=lines)
+    part = width // PARTS
+    spread = [{0: hidden[:, c * part:(c + 1) * part]} for c in range(PARTS)]
+
+    def hop(c, bits):
+        for d in range(line):
+            if bin(d).count("1") == bits:
+                low = d & -d
+                spread[c][d] = line_swap(spread[c][d - low], low)
+
+    hop(0, 1)
 
     routes = routing[:, 0]
     row_ids = jnp.arange(rows_dev)
@@ -113,17 +118,28 @@
     ).astype(BF16)
     normed = (scaled * gain).astype(BF16).reshape(twos + (features // tensor_count, capacity))
 
+    grad, spread = together((grad, spread))
+    hop(1, 1)
     shares = tensor_split(grad.reshape((dp_count,) + twos + (share, capacity)), far_step)
+    shares, spread = together((shares, spread))
+    hop(0, 2)
+    hop(1, 2)
     shares = tensor_split(shares, near_steps)
     rows = dot(shares.reshape(dp_count * share, -1), pick, CONTRACT_LAST).astype(BF16)
-    rows, normed, kv_t = together((rows.reshape(dp_count, share, rows_dev), normed, kv_grad.T))
+    rows = rows.reshape(dp_count, share, rows_dev)
+    rows, normed, kv_t = together((rows, normed, kv_grad.T))
+
+    sided = rows.reshape(line, 2, share, rows_dev)
+    sided = jnp.where(pair_pos == 0, sided, sided[:, ::-1])
+    got = lax.all_to_all(
+        sided, "dp", split_axis=0, concat_axis=0, tiled=True, axis_index_groups=lines
+    )
     normed = tensor_split(normed, far_step)
     kv_slots = tensor_blocks(kv_t, far_step)
-
-    sided = rows.reshape(line, 2, share, rows_dev)
-    sided = jnp.where(pair_pos == 0, sided, sided[:, ::-1])
-    got = [at(sided, line_pos)]
-    got += [line_shift(at(sided, (line_pos + s) % line), s) for s in range(1, line)]
+    got, normed, kv_slots, spread = together((got, normed, kv_slots, spread))
+    hop(2, 1)
+    got = jnp.take(got, line_pos ^ jnp.arange(line), axis=0).transpose(1, 2, 0, 3).reshape(2, share, line * rows_dev)
+    got = tensor_gather(got, 1, far_step)
     normed = dot(tensor_split(normed, near_steps), pick, CONTRACT_LAST).astype(BF16)
     masked = dot(tensor_blocks(kv_slots, near_steps), pick, CONTRACT_LAST).astype(BF16)
     per_dev = kv_cols // (dp_count * tensor_count)
@@ -131,31 +147,42 @@
     masked = masked.reshape(line, 2, block, rows_dev)
     own = at(masked, pair_pos, 1).reshape(line * block, rows_dev)
     other = at(masked, 1 - pair_pos, 1).reshape(line * block, rows_dev)
-    row_grad = tensor_gather(rows, 1, far_step)
-    got, row_grad, own, normed, sent = together(
-        (got, row_grad, own, normed, jnp.concatenate([other, normed], axis=0))
-    )
-    origin = (line_pos - jnp.arange(line)) % line
-    got = jnp.take(jnp.stack(got), origin, axis=0)
-    got = got.transpose(1, 2, 0, 3).reshape(2, share, line * rows_dev)
-    got = tensor_gather(got, 1, far_step)
+    sent = jnp.concatenate([other, normed], axis=0)
+    got, rows, own, normed, sent, spread = together((got, rows, own, normed, sent, spread))
+    hop(2, 2)
+    hop(3, 1)
+    for bits in range(3, line.bit_length()):
+        for c in range(EARLY):
+            hop(c, bits)
     far = pair_swap(sent)
     grads = tensor_gather(got, 1, near_steps).reshape(2, cols, line * rows_dev)
-    row_grad = tensor_gather(row_grad, 1, near_steps).reshape(features, rows_dev)
+
+    def terms_of(c):
+        rows = jnp.concatenate([spread[c][d] for d in range(line)], axis=0)
+        return rows, (dot(grads[1], rows, ROWS_BY_COLS) * factor).astype(BF16)
+
+    pairs = [terms_of(c) for c in range(EARLY)]
+    held, fars = [p[0] for p in pairs], [p[1] for p in pairs]
+    fars, spread = together((fars, spread))
+    gots = [pair_swap(far_c) for far_c in fars]
+    hop(3, 2)
+    for bits in range(3, line.bit_length()):
+        for c in range(EARLY, PARTS):
+            hop(c, bits)
+    row_grad = tensor_gather(rows, 1, steps).reshape(features, rows_dev)
+    row_grad, fars = together((row_grad, fars))
+    hidden_grad = dot(row_grad, connector, COLS_BY_LAST).astype(BF16)
+    gots[0], spread, hidden_grad = together((gots[0], spread, hidden_grad))
+    pairs = [terms_of(c) for c in range(EARLY, PARTS)]
+    held += [p[0] for p in pairs]
+    gots += [pair_swap(p[1]) for p in pairs]
+    gots[0], own, far = together((gots[0], own, far))
     terms = dot(own, normed, CONTRACT_LAST)
     terms = terms + dot(far[:line * block], far[line * block:], CONTRACT_LAST)
     terms = (terms * factor).reshape(line, block, -1)
-    held, grads, row_grad, terms = together((held, grads, row_grad, terms))
-
-    part = width // PARTS
-    held = [held[:, c * part:(c + 1) * part] for c in range(PARTS)]
-    fars = [(dot(grads[1], rows, ROWS_BY_COLS) * factor).astype(BF16) for rows in held]
-    gots = [pair_swap(far) for far in fars]
-    terms, row_grad, fars[-1] = together((terms, row_grad, fars[-1]))
-    hidden_grad = dot(row_grad, connector, COLS_BY_LAST).astype(BF16)
     kv_out = at(terms, line_pos)
-    for s in range(1, line):
-        kv_out = kv_out + line_shift(at(terms, (line_pos + s) % line).astype(BF16), s).astype(F32)
+    for d in range(1, line):
+        kv_out = kv_out + line_swap(at(terms, line_pos ^ d).astype(BF16), d).astype(F32)
     kv_out = kv_out.reshape(twos + (per_dev, -1))
     for k, step in enumerate(steps):
         own, other = at(kv_out, digit(step)), at(kv_out, 1 - digit(step))
@@ -167,7 +194,6 @@
             jnp.stack([other, own], axis=spot),
         )
     kv_weight_grad = kv_out.reshape(per_dev, features).T
-    gots[1], hidden_grad = together((gots[1], hidden_grad))
     outs = [
         dot(rows, grads[0], COLS_BY_LAST) * factor + got.T.astype(F32)
         for rows, got in zip(held, gots)

time: 166 us -> 158 us (0.952)
  between operations: 14.6 us -> 1.24 us
  starting transfers between devices: 28.3 us -> 39.8 us
  local copies, waits for them, and re-layouts: 8.82 us -> 15.6 us
  waiting for transfers between devices: 67.8 us -> 61.6 us
  matrix products: 33.7 us -> 27.9 us
    ppermute x6 -> x15, waiting for transfers between devices: 2.63 us -> 18.5 us  [line_swap(): return lax.ppermute(array, 'dp', moves)]
    ppermute x6 -> x15, starting transfers between devices: 12.1 us -> 24.2 us  [line_swap(): return lax.ppermute(array, 'dp', moves)]
    ppermute x12, waiting for transfers between devices: 39.8 us -> 28.9 us  [tensor_swap(): lax.ppermute(array, 'tensor', [(i, i ^ step) for i in range(tensor_count)])]
    all_gather x1 -> x0, waiting for transfers between devices: 7.76 us -> none  [on_device(): lax.all_gather(hidden, 'dp', axis=0, tiled=True, axis_index_groups=lines)]
    dot_general x15, matrix products: 33.7 us -> 27.9 us  [dot(): return lax.dot_general(a, b, dims, preferred_element_type=F32)]
    unnamed x17 -> x39, local copies, waits for them, and re-layouts: 2.43 us -> 6.59 us
    ppermute x12, starting transfers between devices: 10.5 us -> 6.65 us  [tensor_swap(): lax.ppermute(array, 'tensor', [(i, i ^ step) for i in range(tensor_count)])]
    all_to_all x0 -> x1, starting transfers between devices: none -> 3.65 us  [on_device(): lax.all_to_all(sided, 'dp', split_axis=0, concat_axis=0, tiled=True, axis...]
  transfers between devices with their start and end apart: 24 -> 33, of which waited for: 13 -> 16; matrix products, arithmetic and copies ran while one was open for 27% -> 31% of each run, Pallas kernels for 0% -> 0%
where the time goes in v4:
time: 158 us
  waiting for transfers between devices  61.6 us (39%)
  starting transfers between devices  39.8 us (25%)
  matrix products  27.9 us (18%)
  local copies, waits for them, and re-layouts  15.6 us (10%)
  other arithmetic  11.6 us (7%)
    ppermute x12, waiting for transfers between devices, tensor_swap(): lax.ppermute(array, 'tensor', [(i, i ^ step) for i in range(tensor_count)])  28.9 us
    dot_general x15, matrix products, dot(): return lax.dot_general(a, b, dims, preferred_element_type=F32)  27.9 us
    ppermute x15, starting transfers between devices, line_swap(): return lax.ppermute(array, 'dp', moves)  24.2 us
    ppermute x15, waiting for transfers between devices, line_swap(): return lax.ppermute(array, 'dp', moves)  18.5 us
    ppermute x5, waiting for transfers between devices, pair_swap(): return lax.ppermute(array, 'dp', [(i, i ^ 1) for i in range(dp_count)])  14.2 us
    ppermute x12, starting transfers between devices, tensor_swap(): lax.ppermute(array, 'tensor', [(i, i ^ step) for i in range(tensor_count)])  6.65 us
    unnamed x39, local copies, waits for them, and re-layouts  6.59 us
    ppermute x5, starting transfers between devices, pair_swap(): return lax.ppermute(array, 'dp', [(i, i ^ 1) for i in range(dp_count)])  5.26 us
  transfers between devices with their start and end apart: 33, of which 16 were waited for; matrix products, arithmetic and copies ran while one was open for 31% of the time, Pallas kernels for 0%

profile of v4, /device:TPU:0, one launch (start us, length us, event | category | flops | bytes accessed | tf_op | source)
XLA Modules:
  0.0 157.7 jit_solution(12624529721550456368)
XLA Ops:
  0.6 2.1 %fusion.49 = (bf16[256,512]{1,0:T(8,128)(2,1)S(1)}, bf16[256,512]{1,0:T(8,128)(2,1)}, bf16[256,512]{1,0:T(8,128)(2,1)S(1)}, bf16[256,512]{1,0:T(8,128)(2,1)S(1)}) fusion(bf16[256,2048]{1,0:T(8,128)(2,1)} %param.7), kind=kLoop, calls=%fused_computation.134 | loop fusion | bytes 2097152 | tf_op jit(solution)/shard_map/slice | solution.py:90
  2.7 3.0 %collective-permute-start = (bf16[256,512]{1,0:T(8,128)(2,1)S(1)}, bf16[256,512]{1,0:T(8,128)(2,1)}, u32[]{:S(2)}, u32[]{:S(2)}) collective-permute-start(bf16[256,512]{1,0:T(8,128)(2,1)S(1)} %get-tuple-element.108), channel_id=1, source_target_pairs={{0,8},{4,12},{8,0},{12,4},{16,24},{20,28},{24,16},{28,20},{1,9},{5... | collective-permute-start | bytes 786440 | tf_op jit(solution)/shard_map/ppermute | solution.py:59
  5.7 2.6 %collective-permute-start.1 = (bf16[256,512]{1,0:T(8,128)(2,1)S(1)}, bf16[256,512]{1,0:T(8,128)(2,1)}, u32[]{:S(2)}, u32[]{:S(2)}) collective-permute-start(bf16[256,512]{1,0:T(8,128)(2,1)S(1)} %get-tuple-element.108), channel_id=1, source_target_pairs={{0,16},{4,20},{8,24},{12,28},{16,0},{20,4},{24,8},{28,12},{1,17},{... | collective-permute-start | bytes 786440 | tf_op jit(solution)/shard_map/ppermute | solution.py:59
  9.5 4.7 %fusion.5 = (f32[128]{0:T(128)S(1)}, f32[3584,128]{1,0:T(8,128)S(1)}) fusion(bf16[128,3584]{0,1:T(8,128)(2,1)S(1)} %copy.19, f32[128]{0:T(128)S(1)} %add_rsqrt_fusion, bf16[3584,1024]{1,0:T(8,128)(2,1)} %param.12, bf16[128,1024]{1,0:T(8,128)(2,1)} %param.13, f32[3584]{0:T(1024)S(1)} %copy-done.11), kind=kOutput, calls=%fused_computation.11 | convolution fusion | flops 941817728 | bytes 10370048 | tf_op jit(solution)/shard_map/dot_general | solution.py:18
  17.7 2.5 %collective-permute-done.1 = bf16[256,512]{1,0:T(8,128)(2,1)} collective-permute-done((bf16[256,512]{1,0:T(8,128)(2,1)S(1)}, bf16[256,512]{1,0:T(8,128)(2,1)}, u32[]{:S(2)}, u32[]{:S(2)}) %collective-permute-start.1) | collective-permute-done | bytes 262176 | tf_op jit(solution)/shard_map/ppermute | solution.py:59
  23.0 2.6 %collective-permute-start.4 = (bf16[256,512]{1,0:T(8,128)(2,1)S(1)}, bf16[256,512]{1,0:T(8,128)(2,1)}, u32[]{:S(2)}, u32[]{:S(2)}) collective-permute-start(bf16[256,512]{1,0:T(8,128)(2,1)S(1)} %copy-done), channel_id=1, source_target_pairs={{0,16},{4,20},{8,24},{12,28},{16,0},{20,4},{24,8},{28,12},{1,17},{... | collective-permute-start | bytes 786440 | tf_op jit(solution)/shard_map/ppermute | solution.py:59
  25.6 4.8 %collective-permute-done.2 = bf16[8,2,112,128]{3,2,1,0:T(8,128)(2,1)S(1)} collective-permute-done((bf16[8,2,112,128]{3,2,1,0:T(8,128)(2,1)}, bf16[8,2,112,128]{3,2,1,0:T(8,128)(2,1)S(1)}, u32[]{:S(2)}, u32[]{:S(2)}) %collective-permute-start.2) | collective-permute-done | bytes 458784 | tf_op jit(solution)/shard_map/ppermute | solution.py:52
  30.5 1.8 %collective-permute-done.3 = bf16[256,512]{1,0:T(8,128)(2,1)S(1)} collective-permute-done((bf16[256,512]{1,0:T(8,128)(2,1)S(1)}, bf16[256,512]{1,0:T(8,128)(2,1)S(1)}, u32[]{:S(2)}, u32[]{:S(2)}) %collective-permute-start.3) | collective-permute-done | bytes 262176 | tf_op jit(solution)/shard_map/ppermute | solution.py:59
  32.4 3.9 %collective-permute-done.4 = bf16[256,512]{1,0:T(8,128)(2,1)} collective-permute-done((bf16[256,512]{1,0:T(8,128)(2,1)S(1)}, bf16[256,512]{1,0:T(8,128)(2,1)}, u32[]{:S(2)}, u32[]{:S(2)}) %collective-permute-start.4) | collective-permute-done | bytes 262176 | tf_op jit(solution)/shard_map/ppermute | solution.py:59
  40.1 3.6 %all-to-all-start = ((bf16[4,2,112,256]{3,2,1,0:T(8,128)(2,1)}), bf16[4,2,112,256]{3,2,1,0:T(8,128)(2,1)S(1)}, u32[]{:S(2)}, u32[]{:S(2)}) async-start(bf16[4,2,112,256]{3,2,1,0:T(8,128)(2,1)} %reverse_select_fusion), calls=%async_computation | async-start | bytes 917504 | tf_op jit(solution)/shard_map/all_to_all | solution.py:134
  45.4 1.9 %collective-permute-start.8 = (bf16[256,512]{1,0:T(8,128)(2,1)}, bf16[256,512]{1,0:T(8,128)(2,1)S(1)}, u32[]{:S(2)}, u32[]{:S(2)}) collective-permute-start(bf16[256,512]{1,0:T(8,128)(2,1)} %collective-permute-done.1), channel_id=1, source_target_pairs={{0,8},{4,12},{8,0},{12,4},{16,24},{20,28},{24,16},{28,20},{1,9},{5... | collective-permute-start | bytes 786440 | tf_op jit(solution)/shard_map/ppermute | solution.py:59
  48.2 1.9 %pad_maximum_fusion.6 = bf16[1024,256]{0,1:T(8,128)(2,1)} fusion(bf16[1024,128]{0,1:T(8,128)(2,1)} %collective-permute-done.7, bf16[1024,128]{0,1:T(8,128)(2,1)} %bitcast.12), kind=kLoop, calls=%fused_computation.56 | loop fusion | flops 1048576 | bytes 1048576 | tf_op jit(solution)/shard_map/concatenate | solution.py:66
  50.1 7.1 %collective-permute-done.6 = bf16[2,896,128]{2,1,0:T(8,128)(2,1)S(1)} collective-permute-done((bf16[2,896,128]{2,1,0:T(8,128)(2,1)S(1)}, bf16[2,896,128]{2,1,0:T(8,128)(2,1)S(1)}, u32[]{:S(2)}, u32[]{:S(2)}) %collective-permute-start.6) | collective-permute-done | bytes 458784 | tf_op jit(solution)/shard_map/ppermute | solution.py:52
  57.2 2.8 %collective-permute-done.8 = bf16[256,512]{1,0:T(8,128)(2,1)S(1)} collective-permute-done((bf16[256,512]{1,0:T(8,128)(2,1)}, bf16[256,512]{1,0:T(8,128)(2,1)S(1)}, u32[]{:S(2)}, u32[]{:S(2)}) %collective-permute-start.8) | collective-permute-done | bytes 262176 | tf_op jit(solution)/shard_map/ppermute | solution.py:59
  60.0 4.9 %collective-permute-done.9 = bf16[256,512]{1,0:T(8,128)(2,1)} collective-permute-done((bf16[256,512]{1,0:T(8,128)(2,1)}, bf16[256,512]{1,0:T(8,128)(2,1)}, u32[]{:S(2)}, u32[]{:S(2)}) %collective-permute-start.9) | collective-permute-done | bytes 262176 | tf_op jit(solution)/shard_map/ppermute | solution.py:59
  69.1 2.4 %collective-permute-start.14 = (bf16[256,512]{1,0:T(8,128)(2,1)S(1)}, bf16[256,512]{1,0:T(8,128)(2,1)}, u32[]{:S(2)}, u32[]{:S(2)}) collective-permute-start(bf16[256,512]{1,0:T(8,128)(2,1)S(1)} %get-tuple-element.136), channel_id=1, source_target_pairs={{0,16},{4,20},{8,24},{12,28},{16,0},{20,4},{24,8},{28,12},{1,17},{... | collective-permute-start | bytes 786440 | tf_op jit(solution)/shard_map/ppermute | solution.py:59
  72.2 5.3 %collective-permute-done.10 = bf16[2,112,1024]{2,1,0:T(8,128)(2,1)} collective-permute-done((bf16[2,112,1024]{2,1,0:T(8,128)(2,1)S(1)}, bf16[2,112,1024]{2,1,0:T(8,128)(2,1)}, u32[]{:S(2)}, u32[]{:S(2)}) %collective-permute-start.10) | collective-permute-done | bytes 458784 | tf_op jit(solution)/shard_map/ppermute | solution.py:52
  85.0 2.7 %collective-permute-start.18 = (bf16[256,512]{1,0:T(8,128)(2,1)S(1)}, bf16[256,512]{1,0:T(8,128)(2,1)}, u32[]{:S(2)}, u32[]{:S(2)}) collective-permute-start(bf16[256,512]{1,0:T(8,128)(2,1)S(1)} %get-tuple-element.140), channel_id=1, source_target_pairs={{0,16},{4,20},{8,24},{12,28},{16,0},{20,4},{24,8},{28,12},{1,17},{... | collective-permute-start | bytes 786440 | tf_op jit(solution)/shard_map/ppermute | solution.py:59
  93.1 5.3 %collective-permute-done.21 = bf16[8,112,256]{2,1,0:T(8,128)(2,1)S(1)} collective-permute-done((bf16[8,112,256]{2,1,0:T(8,128)(2,1)S(1)}, bf16[8,112,256]{2,1,0:T(8,128)(2,1)S(1)}, u32[]{:S(2)}, u32[]{:S(2)}) %collective-permute-start.21) | collective-permute-done | bytes 458784 | tf_op jit(solution)/shard_map/ppermute | solution.py:52
  106.3 8.5 %convolution_convert_fusion = bf16[256,2048]{1,0:T(8,128)(2,1)} fusion(bf16[3584,256]{1,0:T(8,128)(2,1)S(1)} %bitcast.126, bf16[2048,3584]{1,0:T(8,128)(2,1)} %param.8), kind=kOutput, calls=%fused_computation.3 | convolution fusion | flops 3758620672 | bytes 17563648 | tf_op jit(solution)/shard_map/dot_general | solution.py:18
  114.8 12.8 %collective-permute-done.19 = bf16[448,512]{1,0:T(8,128)(2,1)} collective-permute-done((bf16[448,512]{1,0:T(8,128)(2,1)}, bf16[448,512]{1,0:T(8,128)(2,1)}, u32[]{:S(2)}, u32[]{:S(2)}) %collective-permute-start.19) | collective-permute-done | bytes 458784 | tf_op jit(solution)/shard_map/ppermute | solution.py:55
  130.6 3.6 %collective-permute-start.29 = (bf16[128,896]{1,0:T(8,128)(2,1)S(1)}, bf16[128,896]{1,0:T(8,128)(2,1)S(1)}, u32[]{:S(2)}, u32[]{:S(2)}) collective-permute-start(bf16[128,896]{1,0:T(8,128)(2,1)S(1)} %get-tuple-element.148), channel_id=1, source_target_pairs={{0,24},{4,28},{8,16},{12,20},{16,8},{20,12},{24,0},{28,4},{1,25},{... | collective-permute-start | bytes 688136 | tf_op jit(solution)/shard_map/ppermute | solution.py:59
  146.3 4.1 %collective-permute-done.30 = f32[2,32,896]{2,1,0:T(8,128)S(1)} collective-permute-done((f32[2,32,896]{2,1,0:T(8,128)S(1)}, f32[2,32,896]{2,1,0:T(8,128)S(1)}, u32[]{:S(2)}, u32[]{:S(2)}) %collective-permute-start.30) | collective-permute-done | bytes 229408 | tf_op jit(solution)/shard_map/ppermute | solution.py:52
  154.1 2.2 %pad_maximum_fusion = f32[2048,448]{0,1:T(8,128)} fusion(f32[512,448]{0,1:T(8,128)S(1)} %fusion.10, f32[512,448]{0,1:T(8,128)S(1)} %fusion.11, f32[512,448]{0,1:T(8,128)S(1)} %fusion.12, f32[512,448]{0,1:T(8,128)S(1)} %fusion.13), kind=kLoop, calls=%fused_computation.2 | loop fusion | flops 2752512 | bytes 7340032 | tf_op jit(solution)/shard_map/concatenate | solution.py:201
  (141 shorter events, 59.4 us)
Async XLA Ops:
  2.7 14.9 %collective-permute-start = (bf16[256,512]{1,0:T(8,128)(2,1)S(1)}, bf16[256,512]{1,0:T(8,128)(2,1)}, u32[]{:S(2)}, u32[]{:S(2)}) collective-permute-start(bf16[256,512]{1,0:T(8,128)(2,1)S(1)} %get-tuple-element.108), channel_id=1, source_target_pairs={{0,8},{4,12},{8,0},{12,4},{16,24},{20,28},{24,16},{28,20},{1,9},{5... | collective-permute-start | bytes 786440 | tf_op jit(solution)/shard_map/ppermute | solution.py:59
  5.7 14.4 %collective-permute-start.1 = (bf16[256,512]{1,0:T(8,128)(2,1)S(1)}, bf16[256,512]{1,0:T(8,128)(2,1)}, u32[]{:S(2)}, u32[]{:S(2)}) collective-permute-start(bf16[256,512]{1,0:T(8,128)(2,1)S(1)} %get-tuple-element.108), channel_id=1, source_target_pairs={{0,16},{4,20},{8,24},{12,28},{16,0},{20,4},{24,8},{28,12},{1,17},{... | collective-permute-start | bytes 786440 | tf_op jit(solution)/shard_map/ppermute | solution.py:59
  23.0 13.2 %collective-permute-start.4 = (bf16[256,512]{1,0:T(8,128)(2,1)S(1)}, bf16[256,512]{1,0:T(8,128)(2,1)}, u32[]{:S(2)}, u32[]{:S(2)}) collective-permute-start(bf16[256,512]{1,0:T(8,128)(2,1)S(1)} %copy-done), channel_id=1, source_target_pairs={{0,16},{4,20},{8,24},{12,28},{16,0},{20,4},{24,8},{28,12},{1,17},{... | collective-permute-start | bytes 786440 | tf_op jit(solution)/shard_map/ppermute | solution.py:59
  40.1 24.8 %all-to-all-start = ((bf16[4,2,112,256]{3,2,1,0:T(8,128)(2,1)}), bf16[4,2,112,256]{3,2,1,0:T(8,128)(2,1)S(1)}, u32[]{:S(2)}, u32[]{:S(2)}) async-start(bf16[4,2,112,256]{3,2,1,0:T(8,128)(2,1)} %reverse_select_fusion), calls=%async_computation | async-start | bytes 917504 | tf_op jit(solution)/shard_map/all_to_all | solution.py:134
  43.8 13.3 %collective-permute-start.6 = (bf16[2,896,128]{2,1,0:T(8,128)(2,1)S(1)}, bf16[2,896,128]{2,1,0:T(8,128)(2,1)S(1)}, u32[]{:S(2)}, u32[]{:S(2)}) collective-permute-start(bf16[2,896,128]{2,1,0:T(8,128)(2,1)S(1)} %get-tuple-element.163), channel_id=1, source_target_pairs={{0,2},{1,3},{2,0},{3,1},{4,6},{5,7},{6,4},{7,5},{8,10},{9,11},{10,... | collective-permute-start | bytes 1376264 | tf_op jit(solution)/shard_map/ppermute | solution.py:52
  45.4 14.6 %collective-permute-start.8 = (bf16[256,512]{1,0:T(8,128)(2,1)}, bf16[256,512]{1,0:T(8,128)(2,1)S(1)}, u32[]{:S(2)}, u32[]{:S(2)}) collective-permute-start(bf16[256,512]{1,0:T(8,128)(2,1)} %collective-permute-done.1), channel_id=1, source_target_pairs={{0,8},{4,12},{8,0},{12,4},{16,24},{20,28},{24,16},{28,20},{1,9},{5... | collective-permute-start | bytes 786440 | tf_op jit(solution)/shard_map/ppermute | solution.py:59
  47.3 17.6 %collective-permute-start.9 = (bf16[256,512]{1,0:T(8,128)(2,1)}, bf16[256,512]{1,0:T(8,128)(2,1)}, u32[]{:S(2)}, u32[]{:S(2)}) collective-permute-start(bf16[256,512]{1,0:T(8,128)(2,1)} %collective-permute-done.4), channel_id=1, source_target_pairs={{0,8},{4,12},{8,0},{12,4},{16,24},{20,28},{24,16},{28,20},{1,9},{5... | collective-permute-start | bytes 786440 | tf_op jit(solution)/shard_map/ppermute | solution.py:59
  65.7 11.9 %collective-permute-start.10 = (bf16[2,112,1024]{2,1,0:T(8,128)(2,1)S(1)}, bf16[2,112,1024]{2,1,0:T(8,128)(2,1)}, u32[]{:S(2)}, u32[]{:S(2)}) collective-permute-start(bf16[2,112,1024]{2,1,0:T(8,128)(2,1)S(1)} %bitcast.143), channel_id=1, source_target_pairs={{0,2},{1,3},{2,0},{3,1},{4,6},{5,7},{6,4},{7,5},{8,10},{9,11},{10,... | collective-permute-start | bytes 1376264 | tf_op jit(solution)/shard_map/ppermute | solution.py:52
  68.1 10.8 %collective-permute-start.12 = (bf16[896,256]{1,0:T(8,128)(2,1)}, bf16[896,256]{1,0:T(8,128)(2,1)}, u32[]{:S(2)}, u32[]{:S(2)}) collective-permute-start(bf16[896,256]{1,0:T(8,128)(2,1)} %get-tuple-element.161), channel_id=1, source_target_pairs={{0,1},{1,0},{2,3},{3,2},{4,5},{5,4},{6,7},{7,6},{8,9},{9,8},{10,11... | collective-permute-start | bytes 1376264 | tf_op jit(solution)/shard_map/ppermute | solution.py:52
  68.1 12.3 %collective-permute-start.11 = (bf16[1024,256]{0,1:T(8,128)(2,1)}, bf16[1024,256]{0,1:T(8,128)(2,1)}, u32[]{:S(2)}, u32[]{:S(2)}) collective-permute-start(bf16[1024,256]{0,1:T(8,128)(2,1)} %pad_maximum_fusion.6), channel_id=1, source_target_pairs={{0,1},{1,0},{2,3},{3,2},{4,5},{5,4},{6,7},{7,6},{8,9},{9,8},{10,11... | collective-permute-start | bytes 1572872 | tf_op jit(solution)/shard_map/ppermute | solution.py:52
  68.6 14.6 %collective-permute-start.13 = (bf16[256,512]{1,0:T(8,128)(2,1)S(1)}, bf16[256,512]{1,0:T(8,128)(2,1)}, u32[]{:S(2)}, u32[]{:S(2)}) collective-permute-start(bf16[256,512]{1,0:T(8,128)(2,1)S(1)} %get-tuple-element.136), channel_id=1, source_target_pairs={{0,8},{4,12},{8,0},{12,4},{16,24},{20,28},{24,16},{28,20},{1,9},{5... | collective-permute-start | bytes 786440 | tf_op jit(solution)/shard_map/ppermute | solution.py:59
  69.1 14.1 %collective-permute-start.14 = (bf16[256,512]{1,0:T(8,128)(2,1)S(1)}, bf16[256,512]{1,0:T(8,128)(2,1)}, u32[]{:S(2)}, u32[]{:S(2)}) collective-permute-start(bf16[256,512]{1,0:T(8,128)(2,1)S(1)} %get-tuple-element.136), channel_id=1, source_target_pairs={{0,16},{4,20},{8,24},{12,28},{16,0},{20,4},{24,8},{28,12},{1,17},{... | collective-permute-start | bytes 786440 | tf_op jit(solution)/shard_map/ppermute | solution.py:59
  83.2 20.6 %collective-permute-start.17 = (bf16[256,512]{1,0:T(8,128)(2,1)S(1)}, bf16[256,512]{1,0:T(8,128)(2,1)S(1)}, u32[]{:S(2)}, u32[]{:S(2)}) collective-permute-start(bf16[256,512]{1,0:T(8,128)(2,1)S(1)} %get-tuple-element.140), channel_id=1, source_target_pairs={{0,8},{4,12},{8,0},{12,4},{16,24},{20,28},{24,16},{28,20},{1,9},{5... | collective-permute-start | bytes 786440 | tf_op jit(solution)/shard_map/ppermute | solution.py:59
  85.0 18.8 %collective-permute-start.18 = (bf16[256,512]{1,0:T(8,128)(2,1)S(1)}, bf16[256,512]{1,0:T(8,128)(2,1)}, u32[]{:S(2)}, u32[]{:S(2)}) collective-permute-start(bf16[256,512]{1,0:T(8,128)(2,1)S(1)} %get-tuple-element.140), channel_id=1, source_target_pairs={{0,16},{4,20},{8,24},{12,28},{16,0},{20,4},{24,8},{28,12},{1,17},{... | collective-permute-start | bytes 786440 | tf_op jit(solution)/shard_map/ppermute | solution.py:59
  87.7 10.7 %collective-permute-start.21 = (bf16[8,112,256]{2,1,0:T(8,128)(2,1)S(1)}, bf16[8,112,256]{2,1,0:T(8,128)(2,1)S(1)}, u32[]{:S(2)}, u32[]{:S(2)}) collective-permute-start(bf16[8,112,256]{2,1,0:T(8,128)(2,1)S(1)} %bitcast.120), channel_id=1, source_target_pairs={{0,2},{1,3},{2,0},{3,1},{4,6},{5,7},{6,4},{7,5},{8,10},{9,11},{10,... | collective-permute-start | bytes 1376264 | tf_op jit(solution)/shard_map/ppermute | solution.py:52
  88.2 12.1 %collective-permute-start.15 = (bf16[2,2,112,1024]{3,2,0,1:T(8,128)(2,1)S(1)}, bf16[2,2,112,1024]{3,2,0,1:T(8,128)(2,1)S(1)}, u32[]{:S(2)}, u32[]{:S(2)}) collective-permute-start(bf16[2,2,112,1024]{3,2,0,1:T(8,128)(2,1)S(1)} %maximum_select_fusion.2), channel_id=1, source_target_pairs={{0,1},{1,0},{2,3},{3,2},{4,5},{5,4},{6,7},{7,6},{8,9},{9,8},{10,11... | collective-permute-start | bytes 2752520 | tf_op jit(solution)/shard_map/ppermute | solution.py:52
  88.3 15.5 %collective-permute-start.16 = (bf16[256,512]{1,0:T(8,128)(2,1)}, bf16[256,512]{1,0:T(8,128)(2,1)S(1)}, u32[]{:S(2)}, u32[]{:S(2)}) collective-permute-start(bf16[256,512]{1,0:T(8,128)(2,1)} %collective-permute-done.14), channel_id=1, source_target_pairs={{0,8},{4,12},{8,0},{12,4},{16,24},{20,28},{24,16},{28,20},{1,9},{5... | collective-permute-start | bytes 786440 | tf_op jit(solution)/shard_map/ppermute | solution.py:59
  98.4 29.2 %collective-permute-start.23 = (bf16[1408,256]{1,0:T(8,128)(2,1)}, bf16[1408,256]{1,0:T(8,128)(2,1)}, u32[]{:S(2)}, u32[]{:S(2)}) collective-permute-start(bf16[1408,256]{1,0:T(8,128)(2,1)} %pad_maximum_fusion.5), channel_id=1, source_target_pairs={{0,4},{4,0},{8,12},{12,8},{16,20},{20,16},{24,28},{28,24},{1,5},{5... | collective-permute-start | bytes 2162696 | tf_op jit(solution)/shard_map/ppermute | solution.py:55
  103.8 23.9 %collective-permute-start.19 = (bf16[448,512]{1,0:T(8,128)(2,1)}, bf16[448,512]{1,0:T(8,128)(2,1)}, u32[]{:S(2)}, u32[]{:S(2)}) collective-permute-start(bf16[448,512]{1,0:T(8,128)(2,1)} %fusion.14), channel_id=1, source_target_pairs={{0,4},{4,0},{8,12},{12,8},{16,20},{20,16},{24,28},{28,24},{1,5},{5... | collective-permute-start | bytes 1376264 | tf_op jit(solution)/shard_map/ppermute | solution.py:55
  105.1 39.3 %collective-permute-start.24 = (bf16[448,512]{1,0:T(8,128)(2,1)}, bf16[448,512]{1,0:T(8,128)(2,1)}, u32[]{:S(2)}, u32[]{:S(2)}) collective-permute-start(bf16[448,512]{1,0:T(8,128)(2,1)} %fusion.15), channel_id=1, source_target_pairs={{0,4},{4,0},{8,12},{12,8},{16,20},{20,16},{24,28},{28,24},{1,5},{5... | collective-permute-start | bytes 1376264 | tf_op jit(solution)/shard_map/ppermute | solution.py:55
  129.8 13.0 %collective-permute-start.27 = (bf16[128,896]{1,0:T(8,128)(2,1)S(1)}, bf16[128,896]{1,0:T(8,128)(2,1)S(1)}, u32[]{:S(2)}, u32[]{:S(2)}) collective-permute-start(bf16[128,896]{1,0:T(8,128)(2,1)S(1)} %get-tuple-element.147), channel_id=1, source_target_pairs={{0,8},{4,12},{8,0},{12,4},{16,24},{20,28},{24,16},{28,20},{1,9},{5... | collective-permute-start | bytes 688136 | tf_op jit(solution)/shard_map/ppermute | solution.py:59
  130.1 14.1 %collective-permute-start.28 = (bf16[128,896]{1,0:T(8,128)(2,1)S(1)}, bf16[128,896]{1,0:T(8,128)(2,1)S(1)}, u32[]{:S(2)}, u32[]{:S(2)}) collective-permute-start(bf16[128,896]{1,0:T(8,128)(2,1)S(1)} %get-tuple-element.149), channel_id=1, source_target_pairs={{0,16},{4,20},{8,24},{12,28},{16,0},{20,4},{24,8},{28,12},{1,17},{... | collective-permute-start | bytes 688136 | tf_op jit(solution)/shard_map/ppermute | solution.py:59
  130.6 13.6 %collective-permute-start.29 = (bf16[128,896]{1,0:T(8,128)(2,1)S(1)}, bf16[128,896]{1,0:T(8,128)(2,1)S(1)}, u32[]{:S(2)}, u32[]{:S(2)}) collective-permute-start(bf16[128,896]{1,0:T(8,128)(2,1)S(1)} %get-tuple-element.148), channel_id=1, source_target_pairs={{0,24},{4,28},{8,16},{12,20},{16,8},{20,12},{24,0},{28,4},{1,25},{... | collective-permute-start | bytes 688136 | tf_op jit(solution)/shard_map/ppermute | solution.py:59
  136.9 14.5 %collective-permute-start.25 = (bf16[448,512]{1,0:T(8,128)(2,1)S(1)}, bf16[448,512]{1,0:T(8,128)(2,1)S(1)}, u32[]{:S(2)}, u32[]{:S(2)}) collective-permute-start(bf16[448,512]{1,0:T(8,128)(2,1)S(1)} %fusion.16), channel_id=1, source_target_pairs={{0,4},{4,0},{8,12},{12,8},{16,20},{20,16},{24,28},{28,24},{1,5},{5... | collective-permute-start | bytes 1376264 | tf_op jit(solution)/shard_map/ppermute | solution.py:55
  (22 other events, 149.8 us)

commit v5 on v4

--- a/solution.py
+++ b/solution.py
@@ -95,6 +95,9 @@
                 low = d & -d
                 spread[c][d] = line_swap(spread[c][d - low], low)
 
+    def joined(c):
+        return jnp.concatenate([spread[c][d] for d in range(line)], axis=0)
+
     hop(0, 1)
 
     routes = routing[:, 0]
@@ -136,7 +139,7 @@
     )
     normed = tensor_split(normed, far_step)
     kv_slots = tensor_blocks(kv_t, far_step)
-    got, normed, kv_slots, spread = together((got, normed, kv_slots, spread))
+    got, spread = together((got, spread))
     hop(2, 1)
     got = jnp.take(got, line_pos ^ jnp.arange(line), axis=0).transpose(1, 2, 0, 3).reshape(2, share, line * rows_dev)
     got = tensor_gather(got, 1, far_step)
@@ -148,7 +151,10 @@
     own = at(masked, pair_pos, 1).reshape(line * block, rows_dev)
     other = at(masked, 1 - pair_pos, 1).reshape(line * block, rows_dev)
     sent = jnp.concatenate([other, normed], axis=0)
-    got, rows, own, normed, sent, spread = together((got, rows, own, normed, sent, spread))
+    early = [joined(c) for c in range(EARLY)] if line == 4 else None
+    got, rows, own, normed, sent, spread, early = together(
+        (got, rows, own, normed, sent, spread, early)
+    )
     hop(2, 2)
     hop(3, 1)
     for bits in range(3, line.bit_length()):
@@ -157,14 +163,16 @@
     far = pair_swap(sent)
     grads = tensor_gather(got, 1, near_steps).reshape(2, cols, line * rows_dev)
 
-    def terms_of(c):
-        rows = jnp.concatenate([spread[c][d] for d in range(line)], axis=0)
+    if early is None:
+        early = [joined(c) for c in range(EARLY)]
+
+    def terms_of(rows):
         return rows, (dot(grads[1], rows, ROWS_BY_COLS) * factor).astype(BF16)
 
-    pairs = [terms_of(c) for c in range(EARLY)]
+    pairs = [terms_of(rows_c) for rows_c in early]
     held, fars = [p[0] for p in pairs], [p[1] for p in pairs]
-    fars, spread = together((fars, spread))
     gots = [pair_swap(far_c) for far_c in fars]
+    fars, spread, far = together((fars, spread, far))
     hop(3, 2)
     for bits in range(3, line.bit_length()):
         for c in range(EARLY, PARTS):
@@ -173,10 +181,10 @@
     row_grad, fars = together((row_grad, fars))
     hidden_grad = dot(row_grad, connector, COLS_BY_LAST).astype(BF16)
     gots[0], spread, hidden_grad = together((gots[0], spread, hidden_grad))
-    pairs = [terms_of(c) for c in range(EARLY, PARTS)]
+    pairs = [terms_of(joined(c)) for c in range(EARLY, PARTS)]
     held += [p[0] for p in pairs]
     gots += [pair_swap(p[1]) for p in pairs]
-    gots[0], own, far = together((gots[0], own, far))
+    gots[0], own = together((gots[0], own))
     terms = dot(own, normed, CONTRACT_LAST)
     terms = terms + dot(far[:line * block], far[line * block:], CONTRACT_LAST)
     terms = (terms * factor).reshape(line, block, -1)

time: 158 us -> 151 us (0.956)
  waiting for transfers between devices: 61.6 us -> 53.5 us
  other arithmetic: 11.6 us -> 16.6 us
  starting transfers between devices: 39.8 us -> 38 us
  local copies, waits for them, and re-layouts: 15.6 us -> 14 us
    ppermute x5, waiting for transfers between devices: 14.2 us -> 2.75 us  [pair_swap(): return lax.ppermute(array, 'dp', [(i, i ^ 1) for i in range(dp_count)])]
    ppermute x12, waiting for transfers between devices: 28.9 us -> 35 us  [tensor_swap(): lax.ppermute(array, 'tensor', [(i, i ^ step) for i in range(tensor_count)])]
    ppermute x15, starting transfers between devices: 24.2 us -> 21.4 us  [line_swap(): return lax.ppermute(array, 'dp', moves)]
    concatenate x0 -> x1, other arithmetic: none -> 2.79 us  [joined(): return jnp.concatenate([spread[c][d] for d in range(line)], axis=0)]
    ppermute x15, waiting for transfers between devices: 18.5 us -> 15.7 us  [line_swap(): return lax.ppermute(array, 'dp', moves)]
  transfers between devices with their start and end apart: 33 -> 33, of which waited for: 16 -> 14; matrix products, arithmetic and copies ran while one was open for 31% -> 34% of each run, Pallas kernels for 0% -> 0%
where the time goes in v5:
time: 151 us; the launch traced here: 150 us
  waiting for transfers between devices  53.5 us (35%)
  starting transfers between devices  38 us (25%)
  matrix products  26.6 us (18%)
  other arithmetic  16.6 us (11%)
  local copies, waits for them, and re-layouts  14 us (9%)
    ppermute x12, waiting for transfers between devices, tensor_swap(): lax.ppermute(array, 'tensor', [(i, i ^ step) for i in range(tensor_count)])  35 us
    dot_general x15, matrix products, dot(): return lax.dot_general(a, b, dims, preferred_element_type=F32)  26.6 us
    ppermute x15, starting transfers between devices, line_swap(): return lax.ppermute(array, 'dp', moves)  21.4 us
    ppermute x15, waiting for transfers between devices, line_swap(): return lax.ppermute(array, 'dp', moves)  15.7 us
    ppermute x12, starting transfers between devices, tensor_swap(): lax.ppermute(array, 'tensor', [(i, i ^ step) for i in range(tensor_count)])  7.05 us
    ppermute x5, starting transfers between devices, pair_swap(): return lax.ppermute(array, 'dp', [(i, i ^ 1) for i in range(dp_count)])  5.92 us
    unnamed x39, local copies, waits for them, and re-layouts  5.02 us
    all_to_all x1, starting transfers between devices, on_device(): lax.all_to_all(sided, 'dp', split_axis=0, concat_axis=0, tiled=True, axis...  3.65 us
  transfers between devices with their start and end apart: 33, of which 14 were waited for; matrix products, arithmetic and copies ran while one was open for 34% of the time, Pallas kernels for 0%

profile of v5, /device:TPU:0, one launch (start us, length us, event | category | flops | bytes accessed | tf_op | source)
XLA Modules:
  0.0 149.9 jit_solution(15828192137079804791)
XLA Ops:
  0.6 2.2 %fusion.55 = (bf16[256,512]{1,0:T(8,128)(2,1)}, bf16[256,512]{1,0:T(8,128)(2,1)S(1)}, bf16[256,512]{1,0:T(8,128)(2,1)S(1)}, bf16[256,512]{1,0:T(8,128)(2,1)}) fusion(bf16[256,2048]{1,0:T(8,128)(2,1)} %param.7), kind=kLoop, calls=%fused_computation.135 | loop fusion | bytes 2097152 | tf_op jit(solution)/shard_map/slice | solution.py:90
  2.8 3.0 %collective-permute-start = (bf16[256,512]{1,0:T(8,128)(2,1)S(1)}, bf16[256,512]{1,0:T(8,128)(2,1)S(1)}, u32[]{:S(2)}, u32[]{:S(2)}) collective-permute-start(bf16[256,512]{1,0:T(8,128)(2,1)S(1)} %get-tuple-element.84), channel_id=1, source_target_pairs={{0,8},{4,12},{8,0},{12,4},{16,24},{20,28},{24,16},{28,20},{1,9},{5... | collective-permute-start | bytes 786440 | tf_op jit(solution)/shard_map/ppermute | solution.py:59
  5.8 2.6 %collective-permute-start.1 = (bf16[256,512]{1,0:T(8,128)(2,1)S(1)}, bf16[256,512]{1,0:T(8,128)(2,1)}, u32[]{:S(2)}, u32[]{:S(2)}) collective-permute-start(bf16[256,512]{1,0:T(8,128)(2,1)S(1)} %get-tuple-element.84), channel_id=1, source_target_pairs={{0,16},{4,20},{8,24},{12,28},{16,0},{20,4},{24,8},{28,12},{1,17},{... | collective-permute-start | bytes 786440 | tf_op jit(solution)/shard_map/ppermute | solution.py:59
  9.6 4.7 %fusion.5 = (f32[128]{0:T(128)S(1)}, f32[3584,128]{1,0:T(8,128)S(1)}) fusion(bf16[128,3584]{0,1:T(8,128)(2,1)S(1)} %copy.19, f32[128]{0:T(128)S(1)} %add_rsqrt_fusion, bf16[3584,1024]{1,0:T(8,128)(2,1)} %param.12, bf16[128,1024]{1,0:T(8,128)(2,1)S(1)} %copy-done.12, f32[3584]{0:T(1024)S(1)} %copy-done.14), kind=kOutput, calls=%fused_computation.11 | convolution fusion | flops 941817728 | bytes 10370048 | tf_op jit(solution)/shard_map/dot_general | solution.py:18
  17.6 2.6 %collective-permute-done.1 = bf16[256,512]{1,0:T(8,128)(2,1)} collective-permute-done((bf16[256,512]{1,0:T(8,128)(2,1)S(1)}, bf16[256,512]{1,0:T(8,128)(2,1)}, u32[]{:S(2)}, u32[]{:S(2)}) %collective-permute-start.1) | collective-permute-done | bytes 262176 | tf_op jit(solution)/shard_map/ppermute | solution.py:59
  23.1 2.6 %collective-permute-start.4 = (bf16[256,512]{1,0:T(8,128)(2,1)S(1)}, bf16[256,512]{1,0:T(8,128)(2,1)}, u32[]{:S(2)}, u32[]{:S(2)}) collective-permute-start(bf16[256,512]{1,0:T(8,128)(2,1)S(1)} %get-tuple-element.88), channel_id=1, source_target_pairs={{0,16},{4,20},{8,24},{12,28},{16,0},{20,4},{24,8},{28,12},{1,17},{... | collective-permute-start | bytes 786440 | tf_op jit(solution)/shard_map/ppermute | solution.py:59
  25.7 4.8 %collective-permute-done.2 = bf16[8,2,112,128]{3,2,1,0:T(8,128)(2,1)S(1)} collective-permute-done((bf16[8,2,112,128]{3,2,1,0:T(8,128)(2,1)}, bf16[8,2,112,128]{3,2,1,0:T(8,128)(2,1)S(1)}, u32[]{:S(2)}, u32[]{:S(2)}) %collective-permute-start.2) | collective-permute-done | bytes 458784 | tf_op jit(solution)/shard_map/ppermute | solution.py:52
  30.6 1.9 %collective-permute-done.3 = bf16[256,512]{1,0:T(8,128)(2,1)} collective-permute-done((bf16[256,512]{1,0:T(8,128)(2,1)S(1)}, bf16[256,512]{1,0:T(8,128)(2,1)}, u32[]{:S(2)}, u32[]{:S(2)}) %collective-permute-start.3) | collective-permute-done | bytes 262176 | tf_op jit(solution)/shard_map/ppermute | solution.py:59
  32.5 3.7 %collective-permute-done.4 = bf16[256,512]{1,0:T(8,128)(2,1)} collective-permute-done((bf16[256,512]{1,0:T(8,128)(2,1)S(1)}, bf16[256,512]{1,0:T(8,128)(2,1)}, u32[]{:S(2)}, u32[]{:S(2)}) %collective-permute-start.4) | collective-permute-done | bytes 262176 | tf_op jit(solution)/shard_map/ppermute | solution.py:59
  39.6 3.6 %all-to-all-start = ((bf16[4,2,112,256]{3,2,1,0:T(8,128)(2,1)}), bf16[4,2,112,256]{3,2,1,0:T(8,128)(2,1)S(1)}, u32[]{:S(2)}, u32[]{:S(2)}) async-start(bf16[4,2,112,256]{3,2,1,0:T(8,128)(2,1)} %reverse_select_fusion), calls=%async_computation | async-start | bytes 917504 | tf_op jit(solution)/shard_map/all_to_all | solution.py:137
  45.5 1.8 %collective-permute-start.6 = (bf16[256,512]{1,0:T(8,128)(2,1)}, bf16[256,512]{1,0:T(8,128)(2,1)S(1)}, u32[]{:S(2)}, u32[]{:S(2)}) collective-permute-start(bf16[256,512]{1,0:T(8,128)(2,1)} %collective-permute-done.1), channel_id=1, source_target_pairs={{0,8},{4,12},{8,0},{12,4},{16,24},{20,28},{24,16},{28,20},{1,9},{5... | collective-permute-start | bytes 786440 | tf_op jit(solution)/shard_map/ppermute | solution.py:59
  47.6 14.1 %collective-permute-done.9 = bf16[1024,128]{0,1:T(8,128)(2,1)} collective-permute-done((bf16[1024,128]{0,1:T(8,128)(2,1)}, bf16[1024,128]{0,1:T(8,128)(2,1)}, u32[]{:S(2)}, u32[]{:S(2)}) %collective-permute-start.9) | collective-permute-done | bytes 262176 | tf_op jit(solution)/shard_map/ppermute | solution.py:52
  61.7 1.9 %pad_maximum_fusion.7 = bf16[1024,256]{0,1:T(8,128)(2,1)} fusion(bf16[1024,128]{0,1:T(8,128)(2,1)} %collective-permute-done.9, bf16[1024,128]{0,1:T(8,128)(2,1)} %bitcast.145), kind=kLoop, calls=%fused_computation.63 | loop fusion | flops 1048576 | bytes 1048576 | tf_op jit(solution)/shard_map/concatenate | solution.py:66
  66.6 2.4 %collective-permute-start.14 = (bf16[256,512]{1,0:T(8,128)(2,1)}, bf16[256,512]{1,0:T(8,128)(2,1)}, u32[]{:S(2)}, u32[]{:S(2)}) collective-permute-start(bf16[256,512]{1,0:T(8,128)(2,1)} %get-tuple-element.114), channel_id=1, source_target_pairs={{0,16},{4,20},{8,24},{12,28},{16,0},{20,4},{24,8},{28,12},{1,17},{... | collective-permute-start | bytes 786440 | tf_op jit(solution)/shard_map/ppermute | solution.py:59
  71.7 2.8 %pad_maximum_fusion.1 = (bf16[1024,512]{1,0:T(8,128)(2,1)}, bf16[1024,512]{1,0:T(8,128)(2,1)}) fusion(bf16[256,512]{1,0:T(8,128)(2,1)} %copy-done.9, bf16[256,512]{1,0:T(8,128)(2,1)} %collective-permute-done.1, bf16[256,512]{1,0:T(8,128)(2,1)S(1)} %collective-permute-done, bf16[256,512]{1,0:T(8,128)(2,1)S(1)} %get-tuple-element.84, ...), kind=kLoop, calls=%fused_computation.43 | loop fusion | flops 8388608 | bytes 4194304 | tf_op jit(solution)/shard_map/concatenate | solution.py:99
  78.7 4.0 %collective-permute-done.8 = bf16[2,112,1024]{2,1,0:T(8,128)(2,1)} collective-permute-done((bf16[2,112,1024]{2,1,0:T(8,128)(2,1)}, bf16[2,112,1024]{2,1,0:T(8,128)(2,1)}, u32[]{:S(2)}, u32[]{:S(2)}) %collective-permute-start.8) | collective-permute-done | bytes 458784 | tf_op jit(solution)/shard_map/ppermute | solution.py:52
  87.1 7.9 %collective-permute-done.22 = bf16[8,112,256]{2,1,0:T(8,128)(2,1)S(1)} collective-permute-done((bf16[8,112,256]{2,1,0:T(8,128)(2,1)S(1)}, bf16[8,112,256]{2,1,0:T(8,128)(2,1)S(1)}, u32[]{:S(2)}, u32[]{:S(2)}) %collective-permute-start.22) | collective-permute-done | bytes 458784 | tf_op jit(solution)/shard_map/ppermute | solution.py:52
  102.2 2.3 %collective-permute-done.17 = bf16[256,512]{1,0:T(8,128)(2,1)S(1)} collective-permute-done((bf16[256,512]{1,0:T(8,128)(2,1)}, bf16[256,512]{1,0:T(8,128)(2,1)S(1)}, u32[]{:S(2)}, u32[]{:S(2)}) %collective-permute-start.17) | collective-permute-done | bytes 262176 | tf_op jit(solution)/shard_map/ppermute | solution.py:59
  107.8 8.5 %convolution_convert_fusion = bf16[256,2048]{1,0:T(8,128)(2,1)} fusion(bf16[3584,256]{1,0:T(8,128)(2,1)S(1)} %bitcast.126, bf16[2048,3584]{1,0:T(8,128)(2,1)} %param.8), kind=kOutput, calls=%fused_computation.3 | convolution fusion | flops 3758620672 | bytes 17563648 | tf_op jit(solution)/shard_map/dot_general | solution.py:18
  116.3 2.0 %collective-permute-done.16 = bf16[448,512]{1,0:T(8,128)(2,1)} collective-permute-done((bf16[448,512]{1,0:T(8,128)(2,1)}, bf16[448,512]{1,0:T(8,128)(2,1)}, u32[]{:S(2)}, u32[]{:S(2)}) %collective-permute-start.16) | collective-permute-done | bytes 458784 | tf_op jit(solution)/shard_map/ppermute | solution.py:55
  120.0 3.3 %collective-permute-start.29 = (bf16[128,896]{1,0:T(8,128)(2,1)S(1)}, bf16[128,896]{1,0:T(8,128)(2,1)S(1)}, u32[]{:S(2)}, u32[]{:S(2)}) collective-permute-start(bf16[128,896]{1,0:T(8,128)(2,1)S(1)} %get-tuple-element.126), channel_id=1, source_target_pairs={{0,24},{4,28},{8,16},{12,20},{16,8},{20,12},{24,0},{28,4},{1,25},{... | collective-permute-start | bytes 688136 | tf_op jit(solution)/shard_map/ppermute | solution.py:59
  133.7 3.4 %collective-permute-done.28 = bf16[128,896]{1,0:T(8,128)(2,1)S(1)} collective-permute-done((bf16[128,896]{1,0:T(8,128)(2,1)S(1)}, bf16[128,896]{1,0:T(8,128)(2,1)S(1)}, u32[]{:S(2)}, u32[]{:S(2)}) %collective-permute-start.28) | collective-permute-done | bytes 229408 | tf_op jit(solution)/shard_map/ppermute | solution.py:59
  140.7 2.6 %collective-permute-done.30 = f32[2,32,896]{2,1,0:T(8,128)S(1)} collective-permute-done((f32[2,32,896]{2,1,0:T(8,128)S(1)}, f32[2,32,896]{2,1,0:T(8,128)S(1)}, u32[]{:S(2)}, u32[]{:S(2)}) %collective-permute-start.30) | collective-permute-done | bytes 229408 | tf_op jit(solution)/shard_map/ppermute | solution.py:52
  146.4 2.2 %pad_maximum_fusion = f32[2048,448]{0,1:T(8,128)} fusion(f32[512,448]{0,1:T(8,128)S(1)} %fusion.10, f32[512,448]{0,1:T(8,128)S(1)} %fusion.11, f32[512,448]{0,1:T(8,128)S(1)} %fusion.12, f32[512,448]{0,1:T(8,128)S(1)} %fusion.13), kind=kLoop, calls=%fused_computation.2 | loop fusion | flops 2752512 | bytes 7340032 | tf_op jit(solution)/shard_map/concatenate | solution.py:209
  (140 shorter events, 57.7 us)
Async XLA Ops:
  2.8 14.8 %collective-permute-start = (bf16[256,512]{1,0:T(8,128)(2,1)S(1)}, bf16[256,512]{1,0:T(8,128)(2,1)S(1)}, u32[]{:S(2)}, u32[]{:S(2)}) collective-permute-start(bf16[256,512]{1,0:T(8,128)(2,1)S(1)} %get-tuple-element.84), channel_id=1, source_target_pairs={{0,8},{4,12},{8,0},{12,4},{16,24},{20,28},{24,16},{28,20},{1,9},{5... | collective-permute-start | bytes 786440 | tf_op jit(solution)/shard_map/ppermute | solution.py:59
  5.8 14.4 %collective-permute-start.1 = (bf16[256,512]{1,0:T(8,128)(2,1)S(1)}, bf16[256,512]{1,0:T(8,128)(2,1)}, u32[]{:S(2)}, u32[]{:S(2)}) collective-permute-start(bf16[256,512]{1,0:T(8,128)(2,1)S(1)} %get-tuple-element.84), channel_id=1, source_target_pairs={{0,16},{4,20},{8,24},{12,28},{16,0},{20,4},{24,8},{28,12},{1,17},{... | collective-permute-start | bytes 786440 | tf_op jit(solution)/shard_map/ppermute | solution.py:59
  23.1 13.2 %collective-permute-start.4 = (bf16[256,512]{1,0:T(8,128)(2,1)S(1)}, bf16[256,512]{1,0:T(8,128)(2,1)}, u32[]{:S(2)}, u32[]{:S(2)}) collective-permute-start(bf16[256,512]{1,0:T(8,128)(2,1)S(1)} %get-tuple-element.88), channel_id=1, source_target_pairs={{0,16},{4,20},{8,24},{12,28},{16,0},{20,4},{24,8},{28,12},{1,17},{... | collective-permute-start | bytes 786440 | tf_op jit(solution)/shard_map/ppermute | solution.py:59
  39.6 25.4 %all-to-all-start = ((bf16[4,2,112,256]{3,2,1,0:T(8,128)(2,1)}), bf16[4,2,112,256]{3,2,1,0:T(8,128)(2,1)S(1)}, u32[]{:S(2)}, u32[]{:S(2)}) async-start(bf16[4,2,112,256]{3,2,1,0:T(8,128)(2,1)} %reverse_select_fusion), calls=%async_computation | async-start | bytes 917504 | tf_op jit(solution)/shard_map/all_to_all | solution.py:137
  43.3 20.2 %collective-permute-start.11 = (bf16[2,896,128]{2,1,0:T(8,128)(2,1)S(1)}, bf16[2,896,128]{2,1,0:T(8,128)(2,1)S(1)}, u32[]{:S(2)}, u32[]{:S(2)}) collective-permute-start(bf16[2,896,128]{2,1,0:T(8,128)(2,1)S(1)} %get-tuple-element.140), channel_id=1, source_target_pairs={{0,2},{1,3},{2,0},{3,1},{4,6},{5,7},{6,4},{7,5},{8,10},{9,11},{10,... | collective-permute-start | bytes 1376264 | tf_op jit(solution)/shard_map/ppermute | solution.py:52
  43.9 17.8 %collective-permute-start.9 = (bf16[1024,128]{0,1:T(8,128)(2,1)}, bf16[1024,128]{0,1:T(8,128)(2,1)}, u32[]{:S(2)}, u32[]{:S(2)}) collective-permute-start(bf16[1024,128]{0,1:T(8,128)(2,1)} %bitcast.144), channel_id=1, source_target_pairs={{0,2},{1,3},{2,0},{3,1},{4,6},{5,7},{6,4},{7,5},{8,10},{9,11},{10,... | collective-permute-start | bytes 786440 | tf_op jit(solution)/shard_map/ppermute | solution.py:52
  45.5 19.5 %collective-permute-start.6 = (bf16[256,512]{1,0:T(8,128)(2,1)}, bf16[256,512]{1,0:T(8,128)(2,1)S(1)}, u32[]{:S(2)}, u32[]{:S(2)}) collective-permute-start(bf16[256,512]{1,0:T(8,128)(2,1)} %collective-permute-done.1), channel_id=1, source_target_pairs={{0,8},{4,12},{8,0},{12,4},{16,24},{20,28},{24,16},{28,20},{1,9},{5... | collective-permute-start | bytes 786440 | tf_op jit(solution)/shard_map/ppermute | solution.py:59
  47.3 17.7 %collective-permute-start.7 = (bf16[256,512]{1,0:T(8,128)(2,1)}, bf16[256,512]{1,0:T(8,128)(2,1)}, u32[]{:S(2)}, u32[]{:S(2)}) collective-permute-start(bf16[256,512]{1,0:T(8,128)(2,1)} %collective-permute-done.4), channel_id=1, source_target_pairs={{0,8},{4,12},{8,0},{12,4},{16,24},{20,28},{24,16},{28,20},{1,9},{5... | collective-permute-start | bytes 786440 | tf_op jit(solution)/shard_map/ppermute | solution.py:59
  64.5 11.8 %collective-permute-start.12 = (bf16[896,256]{1,0:T(8,128)(2,1)}, bf16[896,256]{1,0:T(8,128)(2,1)}, u32[]{:S(2)}, u32[]{:S(2)}) collective-permute-start(bf16[896,256]{1,0:T(8,128)(2,1)} %get-tuple-element.139), channel_id=1, source_target_pairs={{0,1},{1,0},{2,3},{3,2},{4,5},{5,4},{6,7},{7,6},{8,9},{9,8},{10,11... | collective-permute-start | bytes 1376264 | tf_op jit(solution)/shard_map/ppermute | solution.py:52
  65.0 19.0 %collective-permute-start.13 = (bf16[256,512]{1,0:T(8,128)(2,1)}, bf16[256,512]{1,0:T(8,128)(2,1)}, u32[]{:S(2)}, u32[]{:S(2)}) collective-permute-start(bf16[256,512]{1,0:T(8,128)(2,1)} %get-tuple-element.114), channel_id=1, source_target_pairs={{0,8},{4,12},{8,0},{12,4},{16,24},{20,28},{24,16},{28,20},{1,9},{5... | collective-permute-start | bytes 786440 | tf_op jit(solution)/shard_map/ppermute | solution.py:59
  66.6 17.4 %collective-permute-start.14 = (bf16[256,512]{1,0:T(8,128)(2,1)}, bf16[256,512]{1,0:T(8,128)(2,1)}, u32[]{:S(2)}, u32[]{:S(2)}) collective-permute-start(bf16[256,512]{1,0:T(8,128)(2,1)} %get-tuple-element.114), channel_id=1, source_target_pairs={{0,16},{4,20},{8,24},{12,28},{16,0},{20,4},{24,8},{28,12},{1,17},{... | collective-permute-start | bytes 786440 | tf_op jit(solution)/shard_map/ppermute | solution.py:59
  70.5 12.2 %collective-permute-start.8 = (bf16[2,112,1024]{2,1,0:T(8,128)(2,1)}, bf16[2,112,1024]{2,1,0:T(8,128)(2,1)}, u32[]{:S(2)}, u32[]{:S(2)}) collective-permute-start(bf16[2,112,1024]{2,1,0:T(8,128)(2,1)} %bitcast.50), channel_id=1, source_target_pairs={{0,2},{1,3},{2,0},{3,1},{4,6},{5,7},{6,4},{7,5},{8,10},{9,11},{10,... | collective-permute-start | bytes 1376264 | tf_op jit(solution)/shard_map/ppermute | solution.py:52
  84.6 11.4 %collective-permute-start.15 = (bf16[2,2,112,1024]{3,2,0,1:T(8,128)(2,1)S(1)}, bf16[2,2,112,1024]{3,2,0,1:T(8,128)(2,1)}, u32[]{:S(2)}, u32[]{:S(2)}) collective-permute-start(bf16[2,2,112,1024]{3,2,0,1:T(8,128)(2,1)S(1)} %maximum_select_fusion.2), channel_id=1, source_target_pairs={{0,1},{1,0},{2,3},{3,2},{4,5},{5,4},{6,7},{7,6},{8,9},{9,8},{10,11... | collective-permute-start | bytes 2752520 | tf_op jit(solution)/shard_map/ppermute | solution.py:52
  84.6 21.5 %collective-permute-start.18 = (bf16[256,512]{1,0:T(8,128)(2,1)S(1)}, bf16[256,512]{1,0:T(8,128)(2,1)S(1)}, u32[]{:S(2)}, u32[]{:S(2)}) collective-permute-start(bf16[256,512]{1,0:T(8,128)(2,1)S(1)} %copy-done.3), channel_id=1, source_target_pairs={{0,8},{4,12},{8,0},{12,4},{16,24},{20,28},{24,16},{28,20},{1,9},{5... | collective-permute-start | bytes 786440 | tf_op jit(solution)/shard_map/ppermute | solution.py:59
  85.1 21.4 %collective-permute-start.19 = (bf16[256,512]{1,0:T(8,128)(2,1)S(1)}, bf16[256,512]{1,0:T(8,128)(2,1)}, u32[]{:S(2)}, u32[]{:S(2)}) collective-permute-start(bf16[256,512]{1,0:T(8,128)(2,1)S(1)} %copy-done.3), channel_id=1, source_target_pairs={{0,16},{4,20},{8,24},{12,28},{16,0},{20,4},{24,8},{28,12},{1,17},{... | collective-permute-start | bytes 786440 | tf_op jit(solution)/shard_map/ppermute | solution.py:59
  85.6 20.9 %collective-permute-start.20 = (bf16[1408,256]{1,0:T(8,128)(2,1)}, bf16[1408,256]{1,0:T(8,128)(2,1)S(1)}, u32[]{:S(2)}, u32[]{:S(2)}) collective-permute-start(bf16[1408,256]{1,0:T(8,128)(2,1)} %pad_maximum_fusion.6), channel_id=1, source_target_pairs={{0,4},{4,0},{8,12},{12,8},{16,20},{20,16},{24,28},{28,24},{1,5},{5... | collective-permute-start | bytes 2162696 | tf_op jit(solution)/shard_map/ppermute | solution.py:55
  95.9 11.7 %collective-permute-start.23 = (bf16[8,2,112,256]{3,2,1,0:T(8,128)(2,1)S(1)}, bf16[8,2,112,256]{3,2,1,0:T(8,128)(2,1)S(1)}, u32[]{:S(2)}, u32[]{:S(2)}) collective-permute-start(bf16[8,2,112,256]{3,2,1,0:T(8,128)(2,1)S(1)} %maximum_select_fusion.3), channel_id=1, source_target_pairs={{0,1},{1,0},{2,3},{3,2},{4,5},{5,4},{6,7},{7,6},{8,9},{9,8},{10,11... | collective-permute-start | bytes 2752520 | tf_op jit(solution)/shard_map/ppermute | solution.py:52
  104.5 13.8 %collective-permute-start.16 = (bf16[448,512]{1,0:T(8,128)(2,1)}, bf16[448,512]{1,0:T(8,128)(2,1)}, u32[]{:S(2)}, u32[]{:S(2)}) collective-permute-start(bf16[448,512]{1,0:T(8,128)(2,1)} %fusion.14), channel_id=1, source_target_pairs={{0,4},{4,0},{8,12},{12,8},{16,20},{20,16},{24,28},{28,24},{1,5},{5... | collective-permute-start | bytes 1376264 | tf_op jit(solution)/shard_map/ppermute | solution.py:55
  106.0 32.9 %collective-permute-start.24 = (bf16[448,512]{1,0:T(8,128)(2,1)}, bf16[448,512]{1,0:T(8,128)(2,1)}, u32[]{:S(2)}, u32[]{:S(2)}) collective-permute-start(bf16[448,512]{1,0:T(8,128)(2,1)} %fusion.15), channel_id=1, source_target_pairs={{0,4},{4,0},{8,12},{12,8},{16,20},{20,16},{24,28},{28,24},{1,5},{5... | collective-permute-start | bytes 1376264 | tf_op jit(solution)/shard_map/ppermute | solution.py:55
  118.9 14.0 %collective-permute-start.27 = (bf16[128,896]{1,0:T(8,128)(2,1)S(1)}, bf16[128,896]{1,0:T(8,128)(2,1)S(1)}, u32[]{:S(2)}, u32[]{:S(2)}) collective-permute-start(bf16[128,896]{1,0:T(8,128)(2,1)S(1)} %get-tuple-element.125), channel_id=1, source_target_pairs={{0,8},{4,12},{8,0},{12,4},{16,24},{20,28},{24,16},{28,20},{1,9},{5... | collective-permute-start | bytes 688136 | tf_op jit(solution)/shard_map/ppermute | solution.py:59
  119.5 17.6 %collective-permute-start.28 = (bf16[128,896]{1,0:T(8,128)(2,1)S(1)}, bf16[128,896]{1,0:T(8,128)(2,1)S(1)}, u32[]{:S(2)}, u32[]{:S(2)}) collective-permute-start(bf16[128,896]{1,0:T(8,128)(2,1)S(1)} %get-tuple-element.127), channel_id=1, source_target_pairs={{0,16},{4,20},{8,24},{12,28},{16,0},{20,4},{24,8},{28,12},{1,17},{... | collective-permute-start | bytes 688136 | tf_op jit(solution)/shard_map/ppermute | solution.py:59
  120.0 17.1 %collective-permute-start.29 = (bf16[128,896]{1,0:T(8,128)(2,1)S(1)}, bf16[128,896]{1,0:T(8,128)(2,1)S(1)}, u32[]{:S(2)}, u32[]{:S(2)}) collective-permute-start(bf16[128,896]{1,0:T(8,128)(2,1)S(1)} %get-tuple-element.126), channel_id=1, source_target_pairs={{0,24},{4,28},{8,16},{12,20},{16,8},{20,12},{24,0},{28,4},{1,25},{... | collective-permute-start | bytes 688136 | tf_op jit(solution)/shard_map/ppermute | solution.py:59
  127.0 17.4 %collective-permute-start.25 = (bf16[448,512]{1,0:T(8,128)(2,1)S(1)}, bf16[448,512]{1,0:T(8,128)(2,1)S(1)}, u32[]{:S(2)}, u32[]{:S(2)}) collective-permute-start(bf16[448,512]{1,0:T(8,128)(2,1)S(1)} %fusion.16), channel_id=1, source_target_pairs={{0,4},{4,0},{8,12},{12,8},{16,20},{20,16},{24,28},{28,24},{1,5},{5... | collective-permute-start | bytes 1376264 | tf_op jit(solution)/shard_map/ppermute | solution.py:55
  132.9 12.9 %collective-permute-start.26 = (bf16[448,512]{1,0:T(8,128)(2,1)S(1)}, bf16[448,512]{1,0:T(8,128)(2,1)S(1)}, u32[]{:S(2)}, u32[]{:S(2)}) collective-permute-start(bf16[448,512]{1,0:T(8,128)(2,1)S(1)} %fusion.17), channel_id=1, source_target_pairs={{0,4},{4,0},{8,12},{12,8},{16,20},{20,16},{24,28},{28,24},{1,5},{5... | collective-permute-start | bytes 1376264 | tf_op jit(solution)/shard_map/ppermute | solution.py:55
  (25 other events, 147.3 us)
